TPU v7x, 128 devices: a whole 4x4x4 slice. The times are simulated.
128 devices in a mesh: expert: 32 (over z, y, x_hi), replica: 2 (over core), group: 2 (over x_lo).
Axes of the slice: x: 4 (x_hi: 2, x_lo: 2; x = x_hi * 2 + x_lo), y: 4, z: 4, core: 2. Of those that a mesh axis runs over, the one named last changes fastest.
Arguments:
- tokens: bfloat16 [6144, 4096], P('expert', 'group'), may hold values from -6 to 6
- expert_ids: int32 [6144, 8], P('expert'), may hold values from 0 to 127, all different within a row; in each aligned block of 192 rows (0 to 191, 192 to 383, ...) at most 15 rows name the same one
- route_gates: float32 [6144, 8], P('expert'), may hold values from 0.03 to 0.5
- member_order: int32 [32], replicated, may hold values from 0 to 31, each once
- teach_gate: bfloat16 [32, 1536, 4096], P('expert', 'replica', 'group'), may hold values from -0.09375 to 0.09375
- teach_up: bfloat16 [32, 1536, 4096], P('expert', 'replica', 'group'), may hold values from -0.09375 to 0.09375
- teach_down: bfloat16 [32, 1536, 4096], P('expert', 'replica', 'group'), may hold values from -0.15625 to 0.15625
- stud_gate: bfloat16 [32, 1536, 2048], P('expert', 'replica', 'group'), may hold values from -0.09375 to 0.09375
- stud_up: bfloat16 [32, 1536, 2048], P('expert', 'replica', 'group'), may hold values from -0.09375 to 0.09375
- stud_down: bfloat16 [32, 1536, 2048], P('expert', 'replica', 'group'), may hold values from -0.15625 to 0.15625
Outputs:
- residual: float32 [6144, 4096], P('expert', ('group', 'replica'))
- grad_gate: bfloat16 [32, 1536, 2048], P('expert', 'replica', 'group')
- grad_up: bfloat16 [32, 1536, 2048], P('expert', 'replica', 'group')
- grad_down: bfloat16 [32, 1536, 2048], P('expert', 'replica', 'group')
Inputs may be any that keep to these rules, and one draw needn't show every extreme that they name: `expert_ids`: each row names 8 different experts. Within each aligned block of 192 rows no expert is named by more than 15 rows. Only experts below 32 are in the window. `member_order`: every teacher expert of the window appears once.
All inputs are finite; a program needn't handle non-finite values.
Results may differ from a plain program's by a relative error of at most 0.025.
Values may be sent and summed in bfloat16 or wider, within the bound.
A program may use at most 128 MiB of HBM per device.

v0:
```python
import jax
import jax.numpy as jnp
from jax import lax
from jax.sharding import PartitionSpec as P

CAP = 15


def copy_for_each(shard, axis):
    copies = jnp.broadcast_to(shard, (lax.axis_size(axis), *shard.shape))
    return lax.all_to_all(copies, axis, split_axis=0, concat_axis=0, tiled=True)


def of_everyone(shard, axis):
    everything = copy_for_each(shard, axis)
    return jnp.sum(everything.astype(jnp.float32), axis=0)


def from_partner(block, axis, bit):
    count = lax.axis_size(axis)
    route = []
    for low in range(count):
        high = low | 1 << bit
        if high != low and high < count:
            route += [(low, high), (high, low)]
    return lax.ppermute(block, axis, route)


def split_up(shard, dim, peers):
    shape = shard.shape
    pieces = shard.reshape(*shape[:dim], peers, shape[dim] // peers, *shape[dim + 1 :])
    return jnp.moveaxis(pieces, dim, 0)


def sent_and_summed(shard, axis, dim):
    pieces = split_up(shard, dim, lax.axis_size(axis))
    arrived = lax.all_to_all(pieces, axis, split_axis=0, concat_axis=0, tiled=True)
    return arrived.astype(jnp.float32).sum(axis=0)


def in_order(pieces, dim):
    shape = list(pieces.shape[1:])
    shape[dim] *= pieces.shape[0]
    return jnp.moveaxis(pieces, 0, dim).reshape(shape)


def gathered_copies(shard, axis, dim):
    return in_order(copy_for_each(shard, axis), dim)


def matmul(left_side, right_side):
    return jnp.dot(left_side, right_side, preferred_element_type=jnp.float32)


def across_width(left_side, right_side):
    return lax.dot_general(
        left_side, right_side, (((1,), (1,)), ((), ())), preferred_element_type=jnp.float32
    )


def inner_rows(left_side, right_side):
    return lax.dot_general(
        left_side, right_side, (((0,), (0,)), ((), ())), preferred_element_type=jnp.float32
    )


def slot_tables(expert_ids, route_gates, experts_here, capacity):
    tok_count, top_count = expert_ids.shape
    pair_count = tok_count * top_count
    flat_ids = expert_ids.reshape(pair_count)
    flat_gates = route_gates.reshape(pair_count)
    inside = flat_ids < experts_here
    columns = lax.broadcasted_iota(jnp.int32, (pair_count, experts_here), 1)
    onehot = (flat_ids[:, None] == columns).astype(jnp.int32)
    rank_rows = jnp.sum(onehot * (jnp.cumsum(onehot, axis=0) - 1), axis=1)
    target = jnp.where(inside, flat_ids * capacity + rank_rows, experts_here * capacity)
    slot_table = jnp.full((experts_here * capacity,), pair_count, jnp.int32)
    slot_table = slot_table.at[target].set(jnp.arange(pair_count, dtype=jnp.int32), mode="drop")
    filled = slot_table < pair_count
    clamped = jnp.minimum(slot_table, pair_count - 1)
    token_row = clamped // top_count
    weights = jnp.where(filled, flat_gates[clamped], jnp.zeros((), jnp.float32))
    return (token_row, filled, weights)


def arrange_student(returned, inverse, capacity, columns, narrow):
    owners = returned.shape[0]
    shaped = returned.reshape(owners // 2, 2, 2, capacity, columns, narrow)
    by_place = shaped.transpose(0, 2, 3, 4, 1, 5).reshape(owners, capacity, columns * 2 * narrow)
    return by_place[inverse].reshape(owners * capacity, columns * 2 * narrow).astype(jnp.float32)


def shards(
    tokens,
    expert_ids,
    route_gates,
    member_order,
    teach_gate,
    teach_up,
    teach_down,
    stud_gate,
    stud_up,
    stud_down,
):
    owners = lax.axis_size("expert")
    replicas = lax.axis_size("replica")
    tok_count, half_width = tokens.shape
    block_width = half_width // replicas
    narrow = block_width // 2
    capacity = CAP
    token_row, filled, weights = slot_tables(expert_ids, route_gates, owners, capacity)
    picked = jnp.where(filled[:, None], tokens[token_row], jnp.zeros((), jnp.bfloat16))
    teach_send = picked.reshape(owners, capacity, half_width)
    dest_pairs = jnp.repeat(member_order.reshape(owners // 2, 2), 2, axis=0)
    members = teach_send[dest_pairs].reshape(owners, 2 * capacity, replicas, 2, narrow)
    parity = (jnp.arange(owners) % 2)[:, None, None, None]
    stud_send = jnp.where(parity == 0, members[:, :, :, 0, :], members[:, :, :, 1, :])
    stud_send = stud_send.reshape(owners, 2 * capacity, replicas * narrow)
    teach_rows, stud_rows = (
        lax.all_to_all(teach_send, "expert", split_axis=0, concat_axis=0, tiled=True),
        lax.all_to_all(stud_send, "expert", split_axis=0, concat_axis=0, tiled=True),
    )
    teach_in = teach_rows.reshape(owners * capacity, half_width)
    stud_in = stud_rows.reshape(owners * 2 * capacity, replicas * narrow)
    teach_stack = jnp.stack(
        [across_width(teach_in, teach_gate[0]), across_width(teach_in, teach_up[0])]
    )
    teach_stack = of_everyone(teach_stack.astype(jnp.bfloat16), "group").astype(jnp.float32)
    teach_hidden = (teach_stack[0] * jax.nn.sigmoid(teach_stack[0]) * teach_stack[1]).astype(
        jnp.bfloat16
    )
    teach_part = matmul(teach_hidden, teach_down[0])
    stud_stack = jnp.stack([across_width(stud_in, stud_gate[0]), across_width(stud_in, stud_up[0])])
    stud_stack = of_everyone(stud_stack.astype(jnp.bfloat16), "group").astype(jnp.float32)
    stud_stack = stud_stack + from_partner(stud_stack.astype(jnp.bfloat16), "expert", 0).astype(
        stud_stack.dtype
    )
    gate_pre = stud_stack[0]
    up_pre = stud_stack[1]
    sigmoid_gate = jax.nn.sigmoid(gate_pre)
    stud_hidden = (gate_pre * sigmoid_gate * up_pre).astype(jnp.bfloat16)
    stud_part = matmul(stud_hidden, stud_down[0])
    inverse = (
        jnp.zeros((owners,), jnp.int32).at[member_order].set(jnp.arange(owners, dtype=jnp.int32))
    )
    slot_rows = lax.broadcasted_iota(jnp.int32, (tok_count, owners * capacity), 0)
    token_onehot = ((token_row[None, :] == slot_rows) & filled[None, :]).astype(jnp.float32)
    teach_back, stud_back = (
        lax.all_to_all(
            teach_part.astype(jnp.bfloat16).reshape(owners, capacity, half_width),
            "expert",
            split_axis=0,
            concat_axis=0,
            tiled=True,
        ),
        lax.all_to_all(
            stud_part.astype(jnp.bfloat16).reshape(owners, 2 * capacity, replicas * narrow),
            "expert",
            split_axis=0,
            concat_axis=0,
            tiled=True,
        ),
    )
    teach_out = teach_back.reshape(owners * capacity, half_width).astype(jnp.float32)
    stud_out = arrange_student(stud_back, inverse, capacity, replicas, narrow)
    term_rows = weights[:, None] * (stud_out - teach_out)
    spread = jnp.dot(
        token_onehot, term_rows, precision=lax.Precision.HIGHEST, preferred_element_type=jnp.float32
    )
    residual = sent_and_summed(
        spread.reshape(tok_count, replicas, block_width).astype(jnp.bfloat16), "replica", 1
    )
    residual = residual.reshape(tok_count, block_width)
    grad_slots = (weights[:, None] * residual[token_row]).astype(jnp.bfloat16)
    grad_slots = grad_slots.reshape(owners, capacity, 2, narrow)[member_order]
    grad_send = grad_slots.reshape(owners // 2, 2, capacity, 2, narrow).transpose(0, 3, 1, 2, 4)
    grad_send = grad_send.reshape(owners, 2 * capacity, narrow)
    grad_in = lax.all_to_all(grad_send, "expert", split_axis=0, concat_axis=0, tiled=True).reshape(
        owners * 2 * capacity, narrow
    )
    down_local = stud_down[0]
    column_piece = gathered_copies(grad_in, "replica", 1)
    back_hidden = across_width(column_piece, down_local)
    down_grad = inner_rows(stud_hidden, column_piece)
    back_hidden, down_grad = (back_hidden, down_grad)
    back_hidden = of_everyone(back_hidden.astype(jnp.bfloat16), "group").astype(jnp.float32)
    back_hidden = back_hidden + from_partner(back_hidden.astype(jnp.bfloat16), "expert", 0).astype(
        back_hidden.dtype
    )
    gate_rows = (
        back_hidden * up_pre * sigmoid_gate * (1.0 + gate_pre * (1.0 - sigmoid_gate))
    ).astype(jnp.bfloat16)
    up_rows = (back_hidden * gate_pre * sigmoid_gate).astype(jnp.bfloat16)
    grad_gate = inner_rows(gate_rows, stud_in).astype(jnp.bfloat16)[None]
    grad_up = inner_rows(up_rows, stud_in).astype(jnp.bfloat16)[None]
    grad_down = down_grad.astype(jnp.bfloat16)[None]
    return (residual, grad_gate, grad_up, grad_down)


def solution(mesh):
    placed = (
        P("expert", "group"),
        P("expert", None),
        P("expert", None),
        P(),
        P("expert", "replica", "group"),
        P("expert", "replica", "group"),
        P("expert", "replica", "group"),
        P("expert", "replica", "group"),
        P("expert", "replica", "group"),
        P("expert", "replica", "group"),
    )
    return jax.shard_map(
        shards,
        mesh=mesh,
        in_specs=placed,
        out_specs=(
            P("expert", ("group", "replica")),
            P("expert", "replica", "group"),
            P("expert", "replica", "group"),
            P("expert", "replica", "group"),
        ),
        check_vma=False,
    )
```

profile of v0, /device:TPU:1, one launch (start us, length us, event | category | flops | bytes accessed | tf_op | source)
XLA Modules:
  0.0 558.1 jit_solution(2100260725456023190)
XLA Ops:
  6.7 15.9 %reduce-window.6 = s32[32,12,128]{2,1,0:T(8,128)S(1)} reduce-window(s32[32,12,128]{2,1,0:T(8,128)} %fusion.62, s32[]{:T(128)} %constant.25.clone.1), window={size=1x1x128 pad=0_0x0_0x127_0}, to_apply=%region_0.0 | reduce-window | flops 6242304 | bytes 393220 | tf_op jit(solution)/shard_map/reduce-window
  24.9 6.3 %scatter_custom_fusion = s32[480]{0:T(512)S(1)} fusion(s32[1536]{0:T(1024)S(1)} %fusion.67, s32[1536]{0:T(1024)S(1)} %iota.27, s32[]{:T(128)} %constant.21.clone.1), kind=kCustom, calls=%fused_computation.110 | custom fusion | bytes 1924 | tf_op jit(solution)/shard_map/scatter | solution.py:78
  31.3 3.1 gather_fusion
  34.6 6.5 %gather_fusion.1 = bf16[480,2048]{1,0:T(8,128)(2,1)} fusion(bf16[192,2048]{1,0:T(8,128)(2,1)} %param.10, s32[1024]{0:T(1024)S(1)} %get-tuple-element.11), kind=kCustom, calls=%fused_computation.1 | custom fusion | bytes 3934080 | tf_op jit(solution)/shard_map/gather | solution.py:112
  41.1 2.9 gather.24
  44.0 3.2 broadcast_select_fusion
  47.1 4.3 gather_fusion.2
  51.5 9.9 %reshape.189 = bf16[32,30,2,2,512]{4,3,2,1,0:T(2,128)(2,1)} reshape(bf16[64,15,2048]{2,1,0:T(8,128)(2,1)} %gather_fusion.2) | data formatting | bytes 7864320 | tf_op jit(solution)/shard_map/reshape | solution.py:115
  61.4 23.6 %slice_reduce_fusion.1 = (bf16[32,30,2,512]{3,2,1,0:T(2,128)(2,1)}, bf16[32,30,2,512]{3,2,1,0:T(2,128)(2,1)}) fusion(bf16[32,30,2,2,512]{4,3,2,1,0:T(2,128)(2,1)} %reshape.189), kind=kLoop, calls=%fused_computation.17 | loop fusion | bytes 7864320 | tf_op jit(solution)/shard_map/slice | solution.py:117
  85.0 5.9 %reshape.274 = bf16[32,30,1024]{2,1,0:T(8,128)(2,1)} reshape(bf16[32,30,2,512]{3,2,1,0:T(2,128)(2,1)} %get-tuple-element.4) | data formatting | bytes 3932160 | tf_op jit(solution)/shard_map/squeeze | solution.py:117
  90.9 5.7 %reshape.275 = bf16[32,30,1024]{2,1,0:T(8,128)(2,1)} reshape(bf16[32,30,2,512]{3,2,1,0:T(2,128)(2,1)} %get-tuple-element.5) | data formatting | bytes 3932160 | tf_op jit(solution)/shard_map/squeeze | solution.py:117
  96.6 6.4 %copy_select_fusion = bf16[32,30,1024]{2,0,1:T(8,128)(2,1)S(1)} fusion(bf16[32,30,1024]{2,1,0:T(8,128)(2,1)} %reshape.275, bf16[32,30,1024]{2,1,0:T(8,128)(2,1)} %reshape.274, pred[32]{0:T(512)(128)(4,1)S(1)} %fusion.72), kind=kLoop, calls=%fused_computation.42 | loop fusion | flops 983040 | bytes 5898272 | tf_op jit(solution)/shard_map/jit(_where)/select_n | solution.py:117
  104.1 41.0 %all_to_all.50 = bf16[32,30,1024]{2,1,0:T(8,128)(2,1)} all-to-all(bf16[32,30,1024]{2,1,0:T(8,128)(2,1)S(1)} %copy.83), channel_id=1, replica_groups=mesh['expert'=32,'replica'=2,'group'=2] {'expert'}, dimensions={0} | all-to-all | bytes 3932160 | tf_op jit(solution)/shard_map/all_to_all | solution.py:121
  145.2 3.7 reshape.190
  148.9 3.9 fusion.36
  155.2 67.5 %all_to_all.51 = bf16[2,2,960,768]{3,2,1,0:T(8,128)(2,1)} all-to-all(bf16[2,2,960,768]{3,2,1,0:T(8,128)(2,1)S(1)} %broadcast_in_dim.85), channel_id=1, replica_groups=mesh['expert'=32,'replica'=2,'group'=2] {'group'}, dimensions={0} | all-to-all | bytes 11796480 | tf_op jit(solution)/shard_map/all_to_all | solution.py:11
  222.6 6.0 %all-to-all-start.3 = ((bf16[32,15,2048]{2,1,0:T(8,128)(2,1)}), bf16[32,15,2048]{2,1,0:T(8,128)(2,1)}, u32[]{:S(2)}, u32[]{:S(2)}) async-start(bf16[32,15,2048]{2,1,0:T(8,128)(2,1)} %broadcast_select_fusion), calls=%async_computation.3 | async-start | bytes 4194304 | tf_op jit(solution)/shard_map/all_to_all | solution.py:120
  228.6 4.4 convert_reduce_fusion
  239.1 18.0 %all-to-all-done.3 = bf16[32,15,2048]{2,1,0:T(8,128)(2,1)} async-done(((bf16[32,15,2048]{2,1,0:T(8,128)(2,1)}), bf16[32,15,2048]{2,1,0:T(8,128)(2,1)}, u32[]{:S(2)}, u32[]{:S(2)}) %all-to-all-start.3) | async-done | bytes 1966112 | tf_op jit(solution)/shard_map/all_to_all | solution.py:120
  257.1 2.9 reshape.194
  259.9 4.4 fusion.51
  268.1 5.3 all-to-all-start.4
  273.4 42.6 %collective-permute-done = bf16[2,960,768]{2,1,0:T(8,128)(2,1)} collective-permute-done((bf16[2,960,768]{2,1,0:T(8,128)(2,1)}, bf16[2,960,768]{2,1,0:T(8,128)(2,1)}, u32[]{:S(2)}, u32[]{:S(2)}) %collective-permute-start) | collective-permute-done | bytes 2949152 | tf_op jit(solution)/shard_map/ppermute | solution.py:26
  316.1 4.1 convert_add_fusion
  323.9 3.0 convolution_convert_fusion
  326.8 3.7 reshape.191
  330.5 14.1 %all-to-all-done.4 = bf16[2,2,480,768]{3,2,1,0:T(8,128)(2,1)} async-done(((bf16[2,2,480,768]{3,2,1,0:T(8,128)(2,1)}), bf16[2,2,480,768]{3,2,1,0:T(8,128)(2,1)}, u32[]{:S(2)}, u32[]{:S(2)}) %all-to-all-start.4) | async-done | bytes 2949152 | tf_op jit(solution)/shard_map/all_to_all | solution.py:11
  344.5 9.7 %all-to-all-start.2 = ((bf16[32,30,1024]{2,1,0:T(8,128)(2,1)}), bf16[32,30,1024]{2,1,0:T(8,128)(2,1)}, u32[]{:S(2)}, u32[]{:S(2)}) async-start(bf16[32,30,1024]{2,1,0:T(8,128)(2,1)} %reshape.191), calls=%async_computation.2 | async-start | bytes 4194304 | tf_op jit(solution)/shard_map/all_to_all | solution.py:156
  356.8 3.0 fusion.18
  359.8 2.8 reshape.195
  362.7 18.7 %all-to-all-done.2 = bf16[32,30,1024]{2,1,0:T(8,128)(2,1)} async-done(((bf16[32,30,1024]{2,1,0:T(8,128)(2,1)}), bf16[32,30,1024]{2,1,0:T(8,128)(2,1)}, u32[]{:S(2)}, u32[]{:S(2)}) %all-to-all-start.2) | async-done | bytes 1966112 | tf_op jit(solution)/shard_map/all_to_all | solution.py:156
  381.3 5.4 all-to-all-start.5
  387.8 4.8 reshape.276
  392.6 3.4 copy.96
  396.0 4.8 reshape.277
  402.8 10.8 %all-to-all-done.5 = bf16[32,15,2048]{2,1,0:T(8,128)(2,1)} async-done(((bf16[32,15,2048]{2,1,0:T(8,128)(2,1)}), bf16[32,15,2048]{2,1,0:T(8,128)(2,1)}, u32[]{:S(2)}, u32[]{:S(2)}) %all-to-all-start.5) | async-done | bytes 1966112 | tf_op jit(solution)/shard_map/all_to_all | solution.py:149
  413.5 5.1 convert_subtract_fusion
  418.6 3.9 sub.28
  426.9 9.0 %all_to_all.52 = bf16[2,192,1,1024]{3,1,2,0:T(8,128)(2,1)S(1)} all-to-all(bf16[2,192,1,1024]{3,1,2,0:T(8,128)(2,1)S(1)} %fusion.48), channel_id=1, replica_groups=mesh['expert'=32,'replica'=2,'group'=2] {'replica'}, dimensions={0} | all-to-all | bytes 1572864 | tf_op jit(solution)/shard_map/all_to_all | solution.py:37
  438.6 3.0 gather.28
  443.3 3.7 gather_fusion.5
  447.5 22.1 %all_to_all.53 = bf16[32,30,512]{2,1,0:T(8,128)(2,1)S(1)} all-to-all(bf16[32,30,512]{2,1,0:T(8,128)(2,1)S(1)} %reshape.278), channel_id=1, replica_groups=mesh['expert'=32,'replica'=2,'group'=2] {'expert'}, dimensions={0} | all-to-all | bytes 1966080 | tf_op jit(solution)/shard_map/all_to_all | solution.py:178
  470.0 6.8 %all_to_all.54 = bf16[2,960,512]{2,1,0:T(8,128)(2,1)S(1)} all-to-all(bf16[2,960,512]{2,1,0:T(8,128)(2,1)S(1)} %broadcast_in_dim.89), channel_id=1, replica_groups=mesh['expert'=32,'replica'=2,'group'=2] {'replica'}, dimensions={0} | all-to-all | bytes 3932160 | tf_op jit(solution)/shard_map/all_to_all | solution.py:11
  480.1 36.2 %all_to_all.55 = bf16[2,960,768]{2,1,0:T(8,128)(2,1)S(1)} all-to-all(bf16[2,960,768]{2,1,0:T(8,128)(2,1)S(1)} %broadcast_in_dim.90), channel_id=1, replica_groups=mesh['expert'=32,'replica'=2,'group'=2] {'group'}, dimensions={0} | all-to-all | bytes 5898240 | tf_op jit(solution)/shard_map/all_to_all | solution.py:11
  518.2 3.0 fusion.27
  521.2 30.0 %collective-permute-done.1 = bf16[960,768]{1,0:T(8,128)(2,1)S(1)} collective-permute-done((bf16[960,768]{1,0:T(8,128)(2,1)S(1)}, bf16[960,768]{1,0:T(8,128)(2,1)S(1)}, u32[]{:S(2)}, u32[]{:S(2)}) %collective-permute-start.1) | collective-permute-done | bytes 1474592 | tf_op jit(solution)/shard_map/ppermute | solution.py:26
  551.2 3.1 fusion.26
  554.3 3.5 fusion.25
  (102 shorter events, 45.9 us)
Async XLA Ops:
  0.6 356.2 %copy-start = (bf16[1,768,2048]{2,1,0:T(8,128)(2,1)S(1)}, bf16[1,768,2048]{2,1,0:T(8,128)(2,1)}, u32[]{:S(2)}) copy-start(bf16[1,768,2048]{2,1,0:T(8,128)(2,1)} %param.16) | copy-start | bytes 9437188
  148.9 3.9 copy-start.5
  148.9 3.9 copy-start.12
  222.6 34.4 %all-to-all-start.3 = ((bf16[32,15,2048]{2,1,0:T(8,128)(2,1)}), bf16[32,15,2048]{2,1,0:T(8,128)(2,1)}, u32[]{:S(2)}, u32[]{:S(2)}) async-start(bf16[32,15,2048]{2,1,0:T(8,128)(2,1)} %broadcast_select_fusion), calls=%async_computation.3 | async-start | bytes 4194304 | tf_op jit(solution)/shard_map/all_to_all | solution.py:120
  233.0 3.4 copy-start.3
  236.4 79.7 %collective-permute-start = (bf16[2,960,768]{2,1,0:T(8,128)(2,1)}, bf16[2,960,768]{2,1,0:T(8,128)(2,1)}, u32[]{:S(2)}, u32[]{:S(2)}) collective-permute-start(bf16[2,960,768]{2,1,0:T(8,128)(2,1)} %convert_element_type.86), channel_id=1, source_target_pairs={{0,4},{4,0},{8,12},{12,8},{16,20},{20,16},{24,28},{28,24},{32,36},... | collective-permute-start | bytes 8847368 | tf_op jit(solution)/shard_map/ppermute | solution.py:26
  259.9 4.4 copy-start.7
  259.9 4.4 copy-start.11
  268.1 76.5 %all-to-all-start.4 = ((bf16[2,2,480,768]{3,2,1,0:T(8,128)(2,1)}), bf16[2,2,480,768]{3,2,1,0:T(8,128)(2,1)}, u32[]{:S(2)}, u32[]{:S(2)}) async-start(bf16[2,2,480,768]{3,2,1,0:T(8,128)(2,1)} %broadcast_in_dim.88), calls=%async_computation.4 | async-start | bytes 5898240 | tf_op jit(solution)/shard_map/all_to_all | solution.py:11
  320.2 2.5 copy-start.4
  320.2 3.6 copy-start.13
  322.7 1.1 copy-start.8
  344.5 36.8 %all-to-all-start.2 = ((bf16[32,30,1024]{2,1,0:T(8,128)(2,1)}), bf16[32,30,1024]{2,1,0:T(8,128)(2,1)}, u32[]{:S(2)}, u32[]{:S(2)}) async-start(bf16[32,30,1024]{2,1,0:T(8,128)(2,1)} %reshape.191), calls=%async_computation.2 | async-start | bytes 4194304 | tf_op jit(solution)/shard_map/all_to_all | solution.py:156
  362.7 24.2 %copy-start.10 = (s32[32]{0:T(128)S(1)}, s32[32]{0:T(128)}, u32[]{:S(2)}) copy-start(s32[32]{0:T(128)} %param.13) | copy-start | bytes 388
  381.3 32.2 %all-to-all-start.5 = ((bf16[32,15,2048]{2,1,0:T(8,128)(2,1)}), bf16[32,15,2048]{2,1,0:T(8,128)(2,1)}, u32[]{:S(2)}, u32[]{:S(2)}) async-start(bf16[32,15,2048]{2,1,0:T(8,128)(2,1)} %reshape.195), calls=%async_computation.5 | async-start | bytes 4194304 | tf_op jit(solution)/shard_map/all_to_all | solution.py:149
  436.0 2.6 copy-start.2
  476.7 1.4 copy-start.14
  516.3 1.9 copy-start.9
  516.8 34.4 %slice-start = ((s8[5898240]{0:T(1024)(128)(4,1)}), s8[4194304]{0:T(1024)(128)(4,1)S(1)}, s32[]{:S(2)}) async-start(s8[5898240]{0:T(1024)(128)(4,1)} %bitcast.144), calls=%async_computation.10 | async-start | bytes 8388608
  516.9 34.3 %slice-start.1 = ((s8[5898240]{0:T(1024)(128)(4,1)}), s8[1703936]{0:T(1024)(128)(4,1)S(1)}, s32[]{:S(2)}) async-start(s8[5898240]{0:T(1024)(128)(4,1)} %bitcast.144), calls=%async_computation.11 | async-start | bytes 3407872
  516.9 34.3 %copy-start.6 = (bf16[960,1024]{1,0:T(8,128)(2,1)S(1)}, bf16[960,1024]{1,0:T(8,128)(2,1)}, u32[]{:S(2)}) copy-start(bf16[960,1024]{1,0:T(8,128)(2,1)} %reshape.190) | copy-start | bytes 5898244
  516.9 34.2 %collective-permute-start.1 = (bf16[960,768]{1,0:T(8,128)(2,1)S(1)}, bf16[960,768]{1,0:T(8,128)(2,1)S(1)}, u32[]{:S(2)}, u32[]{:S(2)}) collective-permute-start(bf16[960,768]{1,0:T(8,128)(2,1)S(1)} %convert_element_type.102), channel_id=1, source_target_pairs={{0,4},{4,0},{8,12},{12,8},{16,20},{20,16},{24,28},{28,24},{32,36},... | collective-permute-start | bytes 4423688 | tf_op jit(solution)/shard_map/ppermute | solution.py:26
  554.3 3.5 copy-start.1
where the time goes:
time: 564 us; the launch traced here: 558 us
  blocking collectives  182 us (32%)
  waiting for transfers between devices  134 us (24%)
  local copies, waits for them, and re-layouts  126 us (22%)
  other arithmetic  52.5 us (9%)
  matrix products  30.9 us (5%)
  starting transfers between devices  30.3 us (5%)
    all_to_all x3, blocking collectives, copy_for_each(): return lax.all_to_all(copies, axis, split_axis=0, concat_axis=0, tiled=True)  110 us
    ppermute x2, waiting for transfers between devices, from_partner(): return lax.ppermute(block, axis, route)  72.6 us
    all_to_all x1, blocking collectives, shards(): lax.all_to_all(stud_send, 'expert', split_axis=0, concat_axis=0, tiled=True)  41 us
    slice x1, local copies, waits for them, and re-layouts, shards(): members[:, :, :, 0, :]  23.6 us
    all_to_all x1, blocking collectives, shards(): lax.all_to_all(grad_send, 'expert', split_axis=0, concat_axis=0, tiled=True)  22.1 us
    all_to_all x1, waiting for transfers between devices, shards(): lax.all_to_all(stud_part.astype(jnp.bfloat16).reshape(owners, 2 * capacit...  18.7 us
    all_to_all x1, waiting for transfers between devices, shards(): lax.all_to_all(teach_send, 'expert', split_axis=0, concat_axis=0, tiled=T...  18 us
    another operation x2, other arithmetic  15.9 us
  transfers between devices with their start and end apart: 6, of which 6 were waited for; matrix products, arithmetic and copies ran while one was open for 10% of the time, Pallas kernels for 0%

commit v1 on v0

v1 whole, which is shorter than its diff:
```python
import jax
import jax.numpy as jnp
from jax import lax
from jax.experimental import pallas as pl
from jax.experimental.pallas import tpu as pltpu
from jax.sharding import PartitionSpec as P

MESH = pl.DeviceIdType.MESH
BF = jnp.bfloat16
F32 = jnp.float32
OWNERS = 32
TOK = 192
SLOT = 16
TR = OWNERS * SLOT
SR = 2 * TR
HALF = SR // 4
HID = 768
COL = 1024
NAR = 512


def nn(a, b):
    return lax.dot_general(a, b, (((1,), (0,)), ((), ())), preferred_element_type=F32)


def nt(a, b):
    return lax.dot_general(a, b, (((1,), (1,)), ((), ())), preferred_element_type=F32)


def tn(a, b):
    return lax.dot_general(a, b, (((0,), (0,)), ((), ())), preferred_element_type=F32)


def hi_lo(v):
    hi = v.astype(BF)
    return hi, (v - hi.astype(F32)).astype(BF)


def body(
    ids,
    gates,
    order,
    tokens,
    tg,
    tu,
    td,
    sg,
    su,
    sd,
    res_o,
    gg_o,
    gu_o,
    gd_o,
    tok_v,
    tg_v,
    tu_v,
    td_v,
    sg_v,
    su_v,
    sd_v,
    t_onehot,
    s_onehot,
    comb,
    s_send,
    t_send,
    s_x,
    t_x,
    s_psend,
    s_pown,
    s_precv,
    t_psend,
    t_pown,
    t_precv,
    s_hid,
    t_hid,
    t_csend,
    t_crecv,
    t_ret,
    t_back,
    s_csend,
    s_crecv,
    s_ret,
    s_back,
    res_v,
    g_send,
    g_x,
    b_send,
    b_own,
    b_recv,
    gr_v,
    ur_v,
    load_sem,
    out_sem,
    a2a_s,
    a2a_r,
    core_s,
    core_r,
    ring_s,
    ring_r,
):
    me = lax.axis_index("expert")
    r = lax.axis_index("replica")
    g = lax.axis_index("group")
    h = lax.rem(me, 2)
    x = h * 2 + g
    pair = me - h
    nr = 1 - r

    def place(e):
        z, y, hh = e // 8, lax.rem(e // 2, 4), lax.rem(e, 2)
        return 8 * lax.rem(z + y, 4) + 2 * z + hh

    def peer(e):
        return {"expert": e, "replica": r, "group": g}

    def ring(p):
        return {"expert": pair + p // 2, "replica": r, "group": lax.rem(p, 2)}

    other_core = {"expert": me, "replica": nr, "group": g}
    partner = {"expert": me, "replica": r, "group": 1 - g}
    mine = place(me)

    def load(n, src, dst):
        return pltpu.make_async_copy(src, dst, load_sem.at[n])

    loads = [
        load(0, tokens.at[:, pl.ds(pl.multiple_of(r * COL, COL), COL)], tok_v),
        load(1, sg.at[0], sg_v),
        load(2, su.at[0], su_v),
        load(3, tg.at[0], tg_v),
        load(4, tu.at[0], tu_v),
        load(5, sd.at[0, :, pl.ds(0, NAR)], sd_v.at[0]),
        load(6, sd.at[0, :, pl.ds(NAR, NAR)], sd_v.at[1]),
        load(7, td.at[0, :, pl.ds(0, COL)], td_v.at[0]),
        load(8, td.at[0, :, pl.ds(COL, COL)], td_v.at[1]),
    ]
    for one in loads:
        one.start()

    barrier = pltpu.get_barrier_semaphore()

    @pl.loop(1, OWNERS)
    def _(k):
        pl.semaphore_signal(
            barrier, inc=1, device_id=peer(lax.rem(me + k, OWNERS)), device_id_type=MESH
        )

    pl.semaphore_signal(barrier, inc=1, device_id=other_core, device_id_type=MESH)
    pl.semaphore_signal(barrier, inc=1, device_id=partner, device_id_type=MESH)
    pl.semaphore_signal(barrier, inc=1, device_id=ring(lax.rem(3 - x, 4)), device_id_type=MESH)
    expert_col = lax.broadcasted_iota(jnp.int32, (TOK, OWNERS), 1)
    member = jnp.zeros((TOK, OWNERS), F32)
    gate = jnp.zeros((TOK, OWNERS), F32)
    for k in range(8):
        same = ids[:, k : k + 1] == expert_col
        member = jnp.where(same, 1.0, member)
        gate = jnp.where(same, gates[:, k : k + 1], gate)
    member_b = member.astype(BF)
    upto = (
        lax.broadcasted_iota(jnp.int32, (TOK, TOK), 1)
        <= lax.broadcasted_iota(jnp.int32, (TOK, TOK), 0)
    ).astype(F32).astype(BF)
    rank = (member * nn(upto, member_b)).astype(BF)
    slot_expert = lax.broadcasted_iota(jnp.int32, (OWNERS, TR), 1) // SLOT
    spread = (slot_expert == lax.broadcasted_iota(jnp.int32, (OWNERS, TR), 0)).astype(F32).astype(BF)
    turn = (lax.broadcasted_iota(jnp.int32, (OWNERS, OWNERS), 0) == order[0:1, :]).astype(F32).astype(BF)
    s_spread = nn(turn, spread).astype(BF)
    want = (lax.rem(lax.broadcasted_iota(jnp.int32, (TOK, TR), 1), SLOT) + 1).astype(F32)
    gate_hi, gate_lo = hi_lo(gate)
    s_hit = nn(rank, s_spread) == want
    t_hit = nn(rank, spread) == want
    s_onehot[...] = jnp.where(s_hit, 1.0, 0.0).astype(BF)
    t_onehot[...] = jnp.where(t_hit, 1.0, 0.0).astype(BF)
    comb[0] = jnp.where(s_hit, nn(gate_hi, s_spread), 0.0).astype(BF)
    comb[1] = jnp.where(s_hit, nn(gate_lo, s_spread), 0.0).astype(BF)
    comb[2] = jnp.where(t_hit, -nn(gate_hi, spread), 0.0).astype(BF)
    comb[3] = jnp.where(t_hit, -nn(gate_lo, spread), 0.0).astype(BF)
    loads[0].wait()
    for part in range(2):
        for hh in range(2):
            s_send[hh, part * 256 : (part + 1) * 256, :] = tn(
                s_onehot[:, part * 256 : (part + 1) * 256], tok_v[:, hh * NAR : (hh + 1) * NAR]
            ).astype(BF)
    pl.semaphore_wait(barrier, OWNERS + 2)

    def scatter(n, src_of, dst):
        @pl.loop(1, OWNERS)
        def _(k):
            e = lax.rem(me + k, OWNERS)
            pltpu.make_async_remote_copy(
                src_ref=src_of(e),
                dst_ref=dst,
                send_sem=a2a_s.at[n],
                recv_sem=a2a_r.at[n],
                device_id=peer(e),
                device_id_type=MESH,
            ).start()

    def all_sent(n, like):
        pltpu.make_async_copy(like, like, a2a_s.at[n]).wait()

    def all_here(n, like):
        pltpu.make_async_copy(like, like, a2a_r.at[n]).wait()

    def rows(e, size):
        return pl.ds(pl.multiple_of(e * size, size), size)

    s_rows, t_rows = rows(mine, 2 * SLOT), rows(mine, SLOT)
    m_rows = rows(me // 2, 2 * SLOT)
    scatter(0, lambda e: s_send.at[lax.rem(e, 2), rows(e // 2, 2 * SLOT)], s_x.at[r, s_rows])
    s_x[r, s_rows, :] = s_send[h, m_rows, :]
    for part in range(2):
        t_send[part * 256 : (part + 1) * 256, :] = tn(
            t_onehot[:, part * 256 : (part + 1) * 256], tok_v[...]
        ).astype(BF)
    scatter(1, lambda e: t_send.at[rows(e, SLOT)], t_x.at[r, t_rows])
    t_x[r, t_rows, :] = t_send[rows(me, SLOT), :]

    def to_core(n, src, dst):
        return pltpu.make_async_remote_copy(
            src_ref=src,
            dst_ref=dst,
            send_sem=core_s.at[n],
            recv_sem=core_r.at[n],
            device_id=other_core,
            device_id_type=MESH,
        )

    def to_ring(n, src, dst, p):
        return pltpu.make_async_remote_copy(
            src_ref=src,
            dst_ref=dst,
            send_sem=ring_s.at[n],
            recv_sem=ring_r.at[n],
            device_id=ring(p),
            device_id_type=MESH,
        )

    pending = []

    def go(copy):
        copy.start()
        pending.append(copy)
        return copy

    hops = (2, 1, 3, 0)
    shares = [lax.rem(x + d, 4) for d in hops]
    all_here(0, s_x.at[0, pl.ds(0, SR - 2 * SLOT)])
    swaps = []
    for i, q in enumerate(shares):
        block = rows(q, HALF)
        swaps.append(go(to_core(i, s_x.at[r, block], s_x.at[r, block])))
    loads[1].wait()
    loads[2].wait()

    s_pres = []
    for i, (d, q) in enumerate(zip(hops, shares)):
        swaps[i].wait_recv()
        block = rows(q, HALF)
        for n, w in enumerate((sg_v, su_v)):
            total = nt(s_x[0, block, :], w[:, :NAR]) + nt(s_x[1, block, :], w[:, NAR:])
            if d:
                s_psend[d - 1, n] = total.astype(BF)
            else:
                s_pown[n] = total
        if d:
            s_pres.append(go(to_ring(d - 1, s_psend.at[d - 1], s_precv.at[3 - d], q)))

    all_here(1, t_x.at[0, pl.ds(0, TR - SLOT)])
    t_swaps = []
    for i, half in enumerate((1 - g, g)):
        block = rows(half, HALF)
        t_swaps.append(go(to_core(4 + i, t_x.at[r, block], t_x.at[r, block])))
    loads[3].wait()
    loads[4].wait()
    for i, half in enumerate((1 - g, g)):
        t_swaps[i].wait_recv()
        block = rows(half, HALF)
        for n, w in enumerate((tg_v, tu_v)):
            total = nt(t_x[0, block, :], w[:, :COL]) + nt(t_x[1, block, :], w[:, COL:])
            if i == 0:
                t_psend[n] = total.astype(BF)
            else:
                t_pown[n] = total
        if i == 0:
            t_pre = go(
                pltpu.make_async_remote_copy(
                    src_ref=t_psend,
                    dst_ref=t_precv,
                    send_sem=ring_s.at[12],
                    recv_sem=ring_r.at[12],
                    device_id=partner,
                    device_id_type=MESH,
                )
            )
    t_pre.wait_recv()
    t_gate = t_pown[0] + t_precv[0].astype(F32)
    t_up = t_pown[1] + t_precv[1].astype(F32)
    own_half = rows(g, HALF)
    other_half = rows(1 - g, HALF)
    t_hid[own_half, :] = (t_gate * jax.nn.sigmoid(t_gate) * t_up).astype(BF)
    t_share = go(
        pltpu.make_async_remote_copy(
            src_ref=t_hid.at[own_half],
            dst_ref=t_hid.at[own_half],
            send_sem=ring_s.at[13],
            recv_sem=ring_r.at[13],
            device_id=partner,
            device_id_type=MESH,
        )
    )

    for one in s_pres:
        one.wait_recv()
    for n in range(2):
        s_pown[n] = (
            s_pown[n]
            + s_precv[0, n].astype(F32)
            + s_precv[1, n].astype(F32)
            + s_precv[2, n].astype(F32)
        )
    s_gate, s_up = s_pown[0], s_pown[1]
    own_share = rows(x, HALF)
    s_hid[own_share, :] = (s_gate * jax.nn.sigmoid(s_gate) * s_up).astype(BF)
    s_shares = []
    for d in (2, 1, 3):
        s_shares.append(
            go(to_ring(2 + d, s_hid.at[own_share], s_hid.at[own_share], lax.rem(x + d, 4)))
        )

    loads[7].wait()
    loads[8].wait()
    t_outs = []
    for i, block in enumerate((own_half, other_half)):
        if i == 1:
            t_share.wait_recv()
        t_csend[block, :] = nn(t_hid[block, :], td_v[nr]).astype(BF)
    t_out = go(to_core(6, t_csend, t_crecv))

    loads[5].wait()
    loads[6].wait()
    s_csend[own_share, :] = nn(s_hid[own_share, :], sd_v[nr]).astype(BF)

    t_out.wait_recv()
    for i in range(2):
        block = pl.ds(i * HALF, HALF)
        t_ret[block, :] = (nn(t_hid[block, :], td_v[r]) + t_crecv[block, :].astype(F32)).astype(BF)
    scatter(2, lambda e: t_ret.at[rows(place(e), SLOT)], t_back.at[rows(me, SLOT)])
    t_back[rows(me, SLOT), :] = t_ret[t_rows, :]

    for d, one in zip((2, 1, 3), s_shares):
        one.wait_recv()
        block = rows(lax.rem(x + 4 - d, 4), HALF)
        s_csend[block, :] = nn(s_hid[block, :], sd_v[nr]).astype(BF)
    s_out = go(to_core(7, s_csend, s_crecv))
    s_out.wait_recv()
    for i in range(4):
        block = pl.ds(i * HALF, HALF)
        s_ret[block, :] = (nn(s_hid[block, :], sd_v[r]) + s_crecv[block, :].astype(F32)).astype(BF)
    scatter(3, lambda e: s_ret.at[rows(place(e), 2 * SLOT)], s_back.at[h, m_rows])
    s_back[h, m_rows, :] = s_ret[s_rows, :]

    all_here(2, t_back.at[pl.ds(0, TR - SLOT)])
    all_here(3, s_x.at[0, pl.ds(0, SR - 2 * SLOT)])
    for hh in range(2):
        wide = slice(hh * NAR, (hh + 1) * NAR)
        back_s, back_t = s_back[hh], t_back[:, wide]
        residual = (
            nn(comb[0], back_s) + nn(comb[1], back_s) + nn(comb[2], back_t) + nn(comb[3], back_t)
        )
        res_v[:, wide] = residual
        res_hi, res_lo = hi_lo(residual)
        for part in range(2):
            tall = slice(part * 256, (part + 1) * 256)
            g_send[hh, tall, :] = (
                tn(comb[0, :, tall], res_hi)
                + tn(comb[0, :, tall], res_lo)
                + tn(comb[1, :, tall], res_hi)
            ).astype(BF)
    scatter(4, lambda e: g_send.at[lax.rem(e, 2), rows(e // 2, 2 * SLOT)], g_x.at[r, s_rows])
    g_x[r, s_rows, :] = g_send[h, m_rows, :]
    out_res = pltpu.make_async_copy(res_v, res_o, out_sem.at[0])
    out_res.start()

    all_here(4, g_x.at[0, pl.ds(0, SR - 2 * SLOT)])
    swaps = []
    for i, q in enumerate(shares):
        block = rows(q, HALF)
        swaps.append(go(to_core(8 + i, g_x.at[r, block], g_x.at[r, block])))
    b_sums = []
    for i, (d, q) in enumerate(zip(hops, shares)):
        swaps[i].wait_recv()
        block = rows(q, HALF)
        total = nt(g_x[0, block, :], sd_v[0]) + nt(g_x[1, block, :], sd_v[1])
        if d:
            b_send[d - 1] = total.astype(BF)
            b_sums.append(go(to_ring(5 + d, b_send.at[d - 1], b_recv.at[3 - d], q)))
        else:
            b_own[...] = total
    for b in range(2):
        for part in range(3):
            tall = slice(part * 256, (part + 1) * 256)
            td_v[0, tall, b * NAR : (b + 1) * NAR] = tn(s_hid[:, tall], g_x[b]).astype(BF)
    out_gd = pltpu.make_async_copy(td_v.at[0], gd_o.at[0], out_sem.at[1])
    out_gd.start()

    for one in b_sums:
        one.wait_recv()
    back = (
        b_own[...] + b_recv[0].astype(F32) + b_recv[1].astype(F32) + b_recv[2].astype(F32)
    )
    s_gate, s_up = s_pown[0], s_pown[1]
    sig = jax.nn.sigmoid(s_gate)
    gr_v[own_share, :] = (back * s_up * sig * (1.0 + s_gate * (1.0 - sig))).astype(BF)
    ur_v[own_share, :] = (back * s_gate * sig).astype(BF)
    row_shares = []
    for buf, n in ((gr_v, 14), (ur_v, 17)):
        for d in (2, 1, 3):
            row_shares.append(
                go(to_ring(n + d - 1, buf.at[own_share], buf.at[own_share], lax.rem(x + d, 4)))
            )

    for n, (buf, out) in enumerate(((gr_v, gg_o), (ur_v, gu_o))):
        for one in row_shares[3 * n : 3 * n + 3]:
            one.wait_recv()
        for b in range(2):
            for part in range(3):
                tall = slice(part * 256, (part + 1) * 256)
                target = td_v.at[1] if n == 0 else sg_v
                target[tall, b * NAR : (b + 1) * NAR] = tn(buf[:, tall], s_x[b]).astype(BF)
        done = pltpu.make_async_copy(td_v.at[1] if n == 0 else sg_v, out.at[0], out_sem.at[2 + n])
        done.start()
        if n == 0:
            out_gg = done
        else:
            out_gu = done

    all_sent(0, s_x.at[0, pl.ds(0, SR - 2 * SLOT)])
    all_sent(1, t_back.at[pl.ds(0, TR - SLOT)])
    all_sent(2, t_back.at[pl.ds(0, TR - SLOT)])
    all_sent(3, s_x.at[0, pl.ds(0, SR - 2 * SLOT)])
    all_sent(4, s_x.at[0, pl.ds(0, SR - 2 * SLOT)])
    for one in pending:
        one.wait_send()
    for one in (out_res, out_gd, out_gg, out_gu):
        one.wait()


def shards(tokens, ids, gates, order, tg, tu, td, sg, su, sd):
    vmem = pl.BlockSpec(memory_space=pltpu.VMEM)
    hbm = pl.BlockSpec(memory_space=pl.ANY)
    dma = pltpu.SemaphoreType.DMA

    def buf(*shape, dtype=BF):
        return pltpu.VMEM(shape, dtype)

    return pl.pallas_call(
        body,
        out_shape=(
            jax.ShapeDtypeStruct((TOK, COL), F32),
            jax.ShapeDtypeStruct((1, HID, COL), BF),
            jax.ShapeDtypeStruct((1, HID, COL), BF),
            jax.ShapeDtypeStruct((1, HID, COL), BF),
        ),
        in_specs=[vmem] * 3 + [hbm] * 7,
        out_specs=(hbm,) * 4,
        scratch_shapes=[
            buf(TOK, COL),
            buf(HID, 2 * COL),
            buf(HID, 2 * COL),
            buf(2, HID, COL),
            buf(HID, COL),
            buf(HID, COL),
            buf(2, HID, NAR),
            buf(TOK, TR),
            buf(TOK, TR),
            buf(4, TOK, TR),
            buf(2, TR, NAR),
            buf(TR, COL),
            buf(2, SR, NAR),
            buf(2, TR, COL),
            buf(3, 2, HALF, HID),
            buf(2, HALF, HID, dtype=F32),
            buf(3, 2, HALF, HID),
            buf(2, HALF, HID),
            buf(2, HALF, HID, dtype=F32),
            buf(2, HALF, HID),
            buf(SR, HID),
            buf(TR, HID),
            buf(TR, COL),
            buf(TR, COL),
            buf(TR, COL),
            buf(TR, COL),
            buf(SR, NAR),
            buf(SR, NAR),
            buf(SR, NAR),
            buf(2, TR, NAR),
            buf(TOK, COL, dtype=F32),
            buf(2, TR, NAR),
            buf(2, SR, NAR),
            buf(3, HALF, HID),
            buf(HALF, HID, dtype=F32),
            buf(3, HALF, HID),
            buf(SR, HID),
            buf(SR, HID),
            dma((9,)),
            dma((4,)),
            dma((5,)),
            dma((5,)),
            dma((12,)),
            dma((12,)),
            dma((20,)),
            dma((20,)),
        ],
        compiler_params=pltpu.CompilerParams(
            collective_id=0, has_side_effects=True, vmem_limit_bytes=60 << 20
        ),
        cost_estimate=pl.CostEstimate(
            flops=16_000_000_000, bytes_accessed=24_000_000, transcendentals=1_000_000
        ),
        name="distill",
    )(ids, gates, order.reshape(1, OWNERS), tokens, tg, tu, td, sg, su, sd)


def solution(mesh):
    weights = P("expert", "replica", "group")
    return jax.shard_map(
        shards,
        mesh=mesh,
        in_specs=(P("expert", "group"), P("expert", None), P("expert", None), P()) + (weights,) * 6,
        out_specs=(P("expert", ("group", "replica")), weights, weights, weights),
        check_vma=False,
    )
```

time: 564 us -> 229 us (0.41)
  Pallas kernels: 0 us -> 217 us
  blocking collectives: 182 us -> 0 us
  waiting for transfers between devices: 134 us -> 0 us
  local copies, waits for them, and re-layouts: 126 us -> 10.2 us
  other arithmetic: 52.5 us -> 0 us
  matrix products: 30.9 us -> 0 us
  starting transfers between devices: 30.3 us -> 0 us
    pallas_call x0 -> x1, Pallas kernels: none -> 217 us  [shards(): pl.pallas_call(body, out_shape=(jax.ShapeDtypeStruct((TOK, COL), F32), ja...]
    all_to_all x6 -> x0, blocking collectives: 182 us -> none  [the longest x3 110 us: copy_for_each(): return lax.all_to_all(copies, axis, split_axis=0, concat_axis=0, tiled=True)]
    ppermute x2 -> x0, waiting for transfers between devices: 72.6 us -> none  [from_partner(): return lax.ppermute(block, axis, route)]
    all_to_all x4 -> x0, waiting for transfers between devices: 61.5 us -> none  [the longest x1 18.7 us: shards(): lax.all_to_all(stud_part.astype(jnp.bfloat16).reshape(owners, 2 * capacit...]
    reshape x16 -> x0, local copies, waits for them, and re-layouts: 38 us -> none  [the longest x1 9.92 us: shards(): teach_send[dest_pairs].reshape(owners, 2 * capacity, replicas, 2, narrow)]
    dot_general x11 -> x0, matrix products: 30.9 us -> none  [the longest x5 13.4 us: across_width(): lax.dot_general(left_side, right_side, (((1,), (1,)), ((), ())), preferre...]
    gather x8 -> x0, local copies, waits for them, and re-layouts: 28.1 us -> none  [the longest x2 9.35 us: shards(): tokens[token_row]]
    all_to_all x4 -> x0, starting transfers between devices: 26.4 us -> none  [the longest x1 9.68 us: shards(): lax.all_to_all(stud_part.astype(jnp.bfloat16).reshape(owners, 2 * capacit...]
  transfers between devices with their start and end apart: 6 -> 0, of which waited for: 6 -> 0; matrix products, arithmetic and copies ran while one was open for 10% -> 0% of each run, Pallas kernels for 0% -> 0%
where the time goes in v1:
time: 229 us; the launch traced here: 228 us
  Pallas kernels  217 us (95%)
  local copies, waits for them, and re-layouts  10.2 us (4%)
    pallas_call x1, Pallas kernels, shards(): pl.pallas_call(body, out_shape=(jax.ShapeDtypeStruct((TOK, COL), F32), ja...  217 us
    unnamed x12, local copies, waits for them, and re-layouts  10.2 us

profile of v1, /device:TPU:1, one launch (start us, length us, event | category | flops | bytes accessed | tf_op | source)
XLA Modules:
  0.0 228.2 jit_solution(7020299629937424710)
XLA Ops:
  0.6 1.5 copy.14.ids
  2.1 1.5 copy.15.gates
  3.5 217.4 %distill.1 = (f32[192,1024]{1,0:T(8,128)}, bf16[1,768,1024]{2,1,0:T(8,128)(2,1)}, bf16[1,768,1024]{2,1,0:T(8,128)(2,1)}, bf16[1,768,1024]{2,1,0:T(8,128)(2,1)}) custom-call(s32[192,8]{1,0:T(8,128)} %copy.14.ids, f32[192,8]{1,0:T(8,128)} %copy.15.gates, s32[1,32]{1,0:T(1,128)} %bitcast.1, bf16[192,2048]{1,0:T(8,128)(2,1)} %tokens.1, ...), custom_call_target="tpu_custom_call" | custom-call | flops 16000000000 | bytes 24000000 | tf_op jit(solution)/shard_map/distill/pallas_call | solution.py:457
  220.9 0.0 copy-start.2
  220.9 2.2 copy.20
  223.1 0.0 copy-done.2
  223.1 0.0 copy-start.1
  223.1 1.1 copy.21
  224.3 0.8 copy-done.1
  225.1 0.0 copy-start
  225.1 1.1 copy.22
  226.3 0.8 copy-done
  227.1 1.1 copy.23
Async XLA Ops:
  220.9 2.2 copy-start.2
  223.1 2.0 copy-start.1
  225.1 2.0 copy-start

commit v2 on v1

--- a/solution.py
+++ b/solution.py
@@ -61,12 +61,14 @@
     t_onehot,
     s_onehot,
     comb,
+    comb_t,
     s_send,
     t_send,
     s_x,
     t_x,
     s_psend,
     s_pown,
+    s_pkeep,
     s_precv,
     t_psend,
     t_pown,
@@ -86,6 +88,7 @@
     g_x,
     b_send,
     b_own,
+    b_keep,
     b_recv,
     gr_v,
     ur_v,
@@ -116,6 +119,8 @@
     def ring(p):
         return {"expert": pair + p // 2, "replica": r, "group": lax.rem(p, 2)}
 
+    right, left, opposite = lax.rem(x + 1, 4), lax.rem(x + 3, 4), lax.rem(x + 2, 4)
+    near, across = h * 2 + 1 - g, 3 - x
     other_core = {"expert": me, "replica": nr, "group": g}
     partner = {"expert": me, "replica": r, "group": 1 - g}
     mine = place(me)
@@ -147,40 +152,33 @@
 
     pl.semaphore_signal(barrier, inc=1, device_id=other_core, device_id_type=MESH)
     pl.semaphore_signal(barrier, inc=1, device_id=partner, device_id_type=MESH)
-    pl.semaphore_signal(barrier, inc=1, device_id=ring(lax.rem(3 - x, 4)), device_id_type=MESH)
-    expert_col = lax.broadcasted_iota(jnp.int32, (TOK, OWNERS), 1)
-    member = jnp.zeros((TOK, OWNERS), F32)
-    gate = jnp.zeros((TOK, OWNERS), F32)
+    pl.semaphore_signal(barrier, inc=1, device_id=ring(across), device_id_type=MESH)
+    expert_row = lax.broadcasted_iota(jnp.int32, (OWNERS, TOK), 0)
+    member = jnp.zeros((OWNERS, TOK), F32)
+    gate = jnp.zeros((OWNERS, TOK), F32)
     for k in range(8):
-        same = ids[:, k : k + 1] == expert_col
+        same = ids[k : k + 1, :] == expert_row
         member = jnp.where(same, 1.0, member)
-        gate = jnp.where(same, gates[:, k : k + 1], gate)
-    member_b = member.astype(BF)
+        gate = jnp.where(same, gates[k : k + 1, :], gate)
     upto = (
-        lax.broadcasted_iota(jnp.int32, (TOK, TOK), 1)
-        <= lax.broadcasted_iota(jnp.int32, (TOK, TOK), 0)
+        lax.broadcasted_iota(jnp.int32, (TOK, TOK), 0)
+        <= lax.broadcasted_iota(jnp.int32, (TOK, TOK), 1)
     ).astype(F32).astype(BF)
-    rank = (member * nn(upto, member_b)).astype(BF)
-    slot_expert = lax.broadcasted_iota(jnp.int32, (OWNERS, TR), 1) // SLOT
-    spread = (slot_expert == lax.broadcasted_iota(jnp.int32, (OWNERS, TR), 0)).astype(F32).astype(BF)
-    turn = (lax.broadcasted_iota(jnp.int32, (OWNERS, OWNERS), 0) == order[0:1, :]).astype(F32).astype(BF)
-    s_spread = nn(turn, spread).astype(BF)
-    want = (lax.rem(lax.broadcasted_iota(jnp.int32, (TOK, TR), 1), SLOT) + 1).astype(F32)
-    gate_hi, gate_lo = hi_lo(gate)
-    s_hit = nn(rank, s_spread) == want
-    t_hit = nn(rank, spread) == want
+    rank = (member * nn(member.astype(BF), upto)).astype(BF)
+    spread = (
+        lax.broadcasted_iota(jnp.int32, (TR, OWNERS), 0) // SLOT
+        == lax.broadcasted_iota(jnp.int32, (TR, OWNERS), 1)
+    ).astype(F32).astype(BF)
+    turn = (
+        lax.broadcasted_iota(jnp.int32, (OWNERS, OWNERS), 0) == order[0:1, :]
+    ).astype(F32).astype(BF)
+    s_spread = nt(spread, turn).astype(BF)
+    want = (lax.rem(lax.broadcasted_iota(jnp.int32, (TR, TOK), 0), SLOT) + 1).astype(F32)
+    s_hit = nn(s_spread, rank) == want
     s_onehot[...] = jnp.where(s_hit, 1.0, 0.0).astype(BF)
-    t_onehot[...] = jnp.where(t_hit, 1.0, 0.0).astype(BF)
-    comb[0] = jnp.where(s_hit, nn(gate_hi, s_spread), 0.0).astype(BF)
-    comb[1] = jnp.where(s_hit, nn(gate_lo, s_spread), 0.0).astype(BF)
-    comb[2] = jnp.where(t_hit, -nn(gate_hi, spread), 0.0).astype(BF)
-    comb[3] = jnp.where(t_hit, -nn(gate_lo, spread), 0.0).astype(BF)
     loads[0].wait()
-    for part in range(2):
-        for hh in range(2):
-            s_send[hh, part * 256 : (part + 1) * 256, :] = tn(
-                s_onehot[:, part * 256 : (part + 1) * 256], tok_v[:, hh * NAR : (hh + 1) * NAR]
-            ).astype(BF)
+    for hh in range(2):
+        s_send[hh] = nn(s_onehot[...], tok_v[:, hh * NAR : (hh + 1) * NAR]).astype(BF)
     pl.semaphore_wait(barrier, OWNERS + 2)
 
     def scatter(n, src_of, dst):
@@ -196,6 +194,24 @@
                 device_id_type=MESH,
             ).start()
 
+    def scatter_share(n, q, src_of, dst):
+        @pl.loop(0, 8)
+        def _(k):
+            turned = lax.rem(k + me, 8)
+            z = turned // 2
+            e = 8 * z + 2 * lax.rem(q + 4 - z, 4) + lax.rem(turned, 2)
+
+            @pl.when(e != me)
+            def _():
+                pltpu.make_async_remote_copy(
+                    src_ref=src_of(e),
+                    dst_ref=dst,
+                    send_sem=a2a_s.at[n],
+                    recv_sem=a2a_r.at[n],
+                    device_id=peer(e),
+                    device_id_type=MESH,
+                ).start()
+
     def all_sent(n, like):
         pltpu.make_async_copy(like, like, a2a_s.at[n]).wait()
 
@@ -209,12 +225,24 @@
     m_rows = rows(me // 2, 2 * SLOT)
     scatter(0, lambda e: s_send.at[lax.rem(e, 2), rows(e // 2, 2 * SLOT)], s_x.at[r, s_rows])
     s_x[r, s_rows, :] = s_send[h, m_rows, :]
-    for part in range(2):
-        t_send[part * 256 : (part + 1) * 256, :] = tn(
-            t_onehot[:, part * 256 : (part + 1) * 256], tok_v[...]
-        ).astype(BF)
+    t_hit = nn(spread, rank) == want
+    t_onehot[...] = jnp.where(t_hit, 1.0, 0.0).astype(BF)
+    t_send[...] = nn(t_onehot[...], tok_v[...]).astype(BF)
     scatter(1, lambda e: t_send.at[rows(e, SLOT)], t_x.at[r, t_rows])
     t_x[r, t_rows, :] = t_send[rows(me, SLOT), :]
+    gate_hi, gate_lo = hi_lo(gate)
+    s_hit = s_onehot[...].astype(F32)
+    t_hit = t_onehot[...].astype(F32)
+    comb[0] = (s_hit * nn(s_spread, gate_hi)).astype(BF)
+    comb[1] = (s_hit * nn(s_spread, gate_lo)).astype(BF)
+    comb[2] = (t_hit * -nn(spread, gate_hi)).astype(BF)
+    comb[3] = (t_hit * -nn(spread, gate_lo)).astype(BF)
+    same_token = (
+        lax.broadcasted_iota(jnp.int32, (TOK, TOK), 0)
+        == lax.broadcasted_iota(jnp.int32, (TOK, TOK), 1)
+    ).astype(F32).astype(BF)
+    for n in range(4):
+        comb_t[n] = nt(same_token, comb[n]).astype(BF)
 
     def to_core(n, src, dst):
         return pltpu.make_async_remote_copy(
@@ -243,28 +271,28 @@
         pending.append(copy)
         return copy
 
-    hops = (2, 1, 3, 0)
-    shares = [lax.rem(x + d, 4) for d in hops]
     all_here(0, s_x.at[0, pl.ds(0, SR - 2 * SLOT)])
+    order_of_shares = (opposite, across, near, x)
     swaps = []
-    for i, q in enumerate(shares):
+    for i, q in enumerate(order_of_shares):
         block = rows(q, HALF)
         swaps.append(go(to_core(i, s_x.at[r, block], s_x.at[r, block])))
     loads[1].wait()
     loads[2].wait()
-
-    s_pres = []
-    for i, (d, q) in enumerate(zip(hops, shares)):
+    across_sums = []
+    for i, q in enumerate(order_of_shares):
         swaps[i].wait_recv()
         block = rows(q, HALF)
         for n, w in enumerate((sg_v, su_v)):
             total = nt(s_x[0, block, :], w[:, :NAR]) + nt(s_x[1, block, :], w[:, NAR:])
-            if d:
-                s_psend[d - 1, n] = total.astype(BF)
+            if i < 2:
+                s_psend[i, n] = total.astype(BF)
+            elif i == 2:
+                s_pkeep[n] = total
             else:
                 s_pown[n] = total
-        if d:
-            s_pres.append(go(to_ring(d - 1, s_psend.at[d - 1], s_precv.at[3 - d], q)))
+        if i < 2:
+            across_sums.append(go(to_ring(i, s_psend.at[i], s_precv.at[i], across)))
 
     all_here(1, t_x.at[0, pl.ds(0, TR - SLOT)])
     t_swaps = []
@@ -293,6 +321,10 @@
                     device_id_type=MESH,
                 )
             )
+    across_sums[0].wait_recv()
+    for n in range(2):
+        s_psend[2, n] = (s_pkeep[n] + s_precv[0, n].astype(F32)).astype(BF)
+    near_sum = go(to_ring(2, s_psend.at[2], s_precv.at[2], near))
     t_pre.wait_recv()
     t_gate = t_pown[0] + t_precv[0].astype(F32)
     t_up = t_pown[1] + t_precv[1].astype(F32)
@@ -310,54 +342,65 @@
         )
     )
 
-    for one in s_pres:
+    loads[7].wait()
+    loads[8].wait()
+    t_csend[own_half, :] = nn(t_hid[own_half, :], td_v[nr]).astype(BF)
+    t_outs = [go(to_core(6, t_csend.at[own_half], t_crecv.at[own_half]))]
+
+    def teacher_back(half, one):
         one.wait_recv()
+        block = rows(half, HALF)
+        t_ret[block, :] = (nn(t_hid[block, :], td_v[r]) + t_crecv[block, :].astype(F32)).astype(BF)
+        for q in (2 * half, 2 * half + 1):
+            scatter_share(2, q, lambda e: t_ret.at[rows(place(e), SLOT)], t_back.at[rows(me, SLOT)])
+
+    across_sums[1].wait_recv()
+    near_sum.wait_recv()
     for n in range(2):
-        s_pown[n] = (
-            s_pown[n]
-            + s_precv[0, n].astype(F32)
-            + s_precv[1, n].astype(F32)
-            + s_precv[2, n].astype(F32)
-        )
+        s_pown[n] = s_pown[n] + s_precv[1, n].astype(F32) + s_precv[2, n].astype(F32)
     s_gate, s_up = s_pown[0], s_pown[1]
     own_share = rows(x, HALF)
     s_hid[own_share, :] = (s_gate * jax.nn.sigmoid(s_gate) * s_up).astype(BF)
-    s_shares = []
-    for d in (2, 1, 3):
-        s_shares.append(
-            go(to_ring(2 + d, s_hid.at[own_share], s_hid.at[own_share], lax.rem(x + d, 4)))
-        )
-
-    loads[7].wait()
-    loads[8].wait()
-    t_outs = []
-    for i, block in enumerate((own_half, other_half)):
-        if i == 1:
-            t_share.wait_recv()
-        t_csend[block, :] = nn(t_hid[block, :], td_v[nr]).astype(BF)
-    t_out = go(to_core(6, t_csend, t_crecv))
+    own_hidden = s_hid.at[own_share]
+    to_near = go(to_ring(3, own_hidden, own_hidden, near))
+    to_across = go(to_ring(4, own_hidden, own_hidden, across))
 
     loads[5].wait()
     loads[6].wait()
-    s_csend[own_share, :] = nn(s_hid[own_share, :], sd_v[nr]).astype(BF)
-
-    t_out.wait_recv()
-    for i in range(2):
-        block = pl.ds(i * HALF, HALF)
-        t_ret[block, :] = (nn(t_hid[block, :], td_v[r]) + t_crecv[block, :].astype(F32)).astype(BF)
-    scatter(2, lambda e: t_ret.at[rows(place(e), SLOT)], t_back.at[rows(me, SLOT)])
+    s_outs = []
+
+    def merged_part(i, q):
+        block = rows(q, HALF)
+        s_csend[block, :] = nn(s_hid[block, :], sd_v[nr]).astype(BF)
+        s_outs.append(go(to_core(8 + i, s_csend.at[block], s_crecv.at[block])))
+
+    def merged_back(i, q):
+        s_outs[i].wait_recv()
+        block = rows(q, HALF)
+        s_ret[block, :] = (nn(s_hid[block, :], sd_v[r]) + s_crecv[block, :].astype(F32)).astype(BF)
+        scatter_share(
+            3, q, lambda e: s_ret.at[rows(place(e), 2 * SLOT)], s_back.at[h, m_rows]
+        )
+
+    t_share.wait_recv()
+    t_csend[other_half, :] = nn(t_hid[other_half, :], td_v[nr]).astype(BF)
+    t_outs.append(go(to_core(7, t_csend.at[other_half], t_crecv.at[other_half])))
+    merged_part(0, x)
+    teacher_back(g, t_outs[0])
+    teacher_back(1 - g, t_outs[1])
     t_back[rows(me, SLOT), :] = t_ret[t_rows, :]
-
-    for d, one in zip((2, 1, 3), s_shares):
-        one.wait_recv()
-        block = rows(lax.rem(x + 4 - d, 4), HALF)
-        s_csend[block, :] = nn(s_hid[block, :], sd_v[nr]).astype(BF)
-    s_out = go(to_core(7, s_csend, s_crecv))
-    s_out.wait_recv()
-    for i in range(4):
-        block = pl.ds(i * HALF, HALF)
-        s_ret[block, :] = (nn(s_hid[block, :], sd_v[r]) + s_crecv[block, :].astype(F32)).astype(BF)
-    scatter(3, lambda e: s_ret.at[rows(place(e), 2 * SLOT)], s_back.at[h, m_rows])
+    to_near.wait_recv()
+    near_hidden = s_hid.at[rows(near, HALF)]
+    passed_on = go(to_ring(5, near_hidden, near_hidden, across))
+    merged_part(1, near)
+    merged_back(0, x)
+    to_across.wait_recv()
+    merged_part(2, across)
+    merged_back(1, near)
+    merged_back(2, across)
+    passed_on.wait_recv()
+    merged_part(3, opposite)
+    merged_back(3, opposite)
     s_back[h, m_rows, :] = s_ret[s_rows, :]
 
     all_here(2, t_back.at[pl.ds(0, TR - SLOT)])
@@ -366,74 +409,110 @@
         wide = slice(hh * NAR, (hh + 1) * NAR)
         back_s, back_t = s_back[hh], t_back[:, wide]
         residual = (
-            nn(comb[0], back_s) + nn(comb[1], back_s) + nn(comb[2], back_t) + nn(comb[3], back_t)
+            nn(comb_t[0], back_s)
+            + nn(comb_t[1], back_s)
+            + nn(comb_t[2], back_t)
+            + nn(comb_t[3], back_t)
         )
         res_v[:, wide] = residual
         res_hi, res_lo = hi_lo(residual)
-        for part in range(2):
-            tall = slice(part * 256, (part + 1) * 256)
-            g_send[hh, tall, :] = (
-                tn(comb[0, :, tall], res_hi)
-                + tn(comb[0, :, tall], res_lo)
-                + tn(comb[1, :, tall], res_hi)
-            ).astype(BF)
+        g_send[hh] = (
+            nn(comb[0], res_hi) + nn(comb[0], res_lo) + nn(comb[1], res_hi)
+        ).astype(BF)
     scatter(4, lambda e: g_send.at[lax.rem(e, 2), rows(e // 2, 2 * SLOT)], g_x.at[r, s_rows])
     g_x[r, s_rows, :] = g_send[h, m_rows, :]
     out_res = pltpu.make_async_copy(res_v, res_o, out_sem.at[0])
     out_res.start()
 
     all_here(4, g_x.at[0, pl.ds(0, SR - 2 * SLOT)])
+    order_of_shares = (opposite, right, left, x)
     swaps = []
-    for i, q in enumerate(shares):
+    for i, q in enumerate(order_of_shares):
         block = rows(q, HALF)
-        swaps.append(go(to_core(8 + i, g_x.at[r, block], g_x.at[r, block])))
-    b_sums = []
-    for i, (d, q) in enumerate(zip(hops, shares)):
+        swaps.append(go(to_core(12 + i, g_x.at[r, block], g_x.at[r, block])))
+    top, low = pl.ds(0, HALF // 2), pl.ds(HALF // 2, HALF // 2)
+    for i, q in enumerate(order_of_shares):
         swaps[i].wait_recv()
         block = rows(q, HALF)
         total = nt(g_x[0, block, :], sd_v[0]) + nt(g_x[1, block, :], sd_v[1])
-        if d:
-            b_send[d - 1] = total.astype(BF)
-            b_sums.append(go(to_ring(5 + d, b_send.at[d - 1], b_recv.at[3 - d], q)))
+        if i == 0:
+            b_send[0] = total.astype(BF)
+            from_left = go(to_ring(6, b_send.at[0, top], b_recv.at[0, top], right))
+            from_right = go(to_ring(7, b_send.at[0, low], b_recv.at[0, low], left))
+        elif i == 1:
+            b_send[1, low, :] = total[HALF // 2 :].astype(BF)
+            b_keep[top, :] = total[: HALF // 2]
+            left_low = go(to_ring(8, b_send.at[1, low], b_recv.at[1, low], right))
+        elif i == 2:
+            b_send[2, top, :] = total[: HALF // 2].astype(BF)
+            b_keep[low, :] = total[HALF // 2 :]
+            right_top = go(to_ring(9, b_send.at[2, top], b_recv.at[2, top], left))
         else:
             b_own[...] = total
-    for b in range(2):
+
+    def down_grad(b):
         for part in range(3):
             tall = slice(part * 256, (part + 1) * 256)
             td_v[0, tall, b * NAR : (b + 1) * NAR] = tn(s_hid[:, tall], g_x[b]).astype(BF)
+
+    down_grad(0)
+    from_left.wait_recv()
+    b_send[1, top, :] = (b_keep[top, :] + b_recv[0, top, :].astype(F32)).astype(BF)
+    left_top = go(to_ring(10, b_send.at[1, top], b_recv.at[1, top], right))
+    from_right.wait_recv()
+    b_send[2, low, :] = (b_keep[low, :] + b_recv[0, low, :].astype(F32)).astype(BF)
+    right_low = go(to_ring(11, b_send.at[2, low], b_recv.at[2, low], left))
+    down_grad(1)
     out_gd = pltpu.make_async_copy(td_v.at[0], gd_o.at[0], out_sem.at[1])
     out_gd.start()
 
-    for one in b_sums:
+    for one in (left_low, right_top, left_top, right_low):
         one.wait_recv()
-    back = (
-        b_own[...] + b_recv[0].astype(F32) + b_recv[1].astype(F32) + b_recv[2].astype(F32)
-    )
+    back = b_own[...] + b_recv[1].astype(F32) + b_recv[2].astype(F32)
     s_gate, s_up = s_pown[0], s_pown[1]
     sig = jax.nn.sigmoid(s_gate)
+
+    def part_of(q, lower):
+        return pl.ds(pl.multiple_of(q * HALF + lower * (HALF // 2), HALF // 2), HALF // 2)
+
+    def share_rows(n, buf):
+        def send(i, q, lower, p):
+            block = buf.at[part_of(q, lower)]
+            return go(to_ring(n + i, block, block, p))
+
+        return send, [send(0, x, 0, right), send(1, x, 1, left)], [
+            send(2, x, 1, right),
+            send(3, x, 0, left),
+        ]
+
+    def pass_rows(send, first):
+        first[0].wait_recv()
+        one = send(4, left, 0, right)
+        first[1].wait_recv()
+        return [one, send(5, right, 1, left)]
+
     gr_v[own_share, :] = (back * s_up * sig * (1.0 + s_gate * (1.0 - sig))).astype(BF)
+    g_sender, g_first, g_rest = share_rows(14, gr_v)
     ur_v[own_share, :] = (back * s_gate * sig).astype(BF)
-    row_shares = []
-    for buf, n in ((gr_v, 14), (ur_v, 17)):
-        for d in (2, 1, 3):
-            row_shares.append(
-                go(to_ring(n + d - 1, buf.at[own_share], buf.at[own_share], lax.rem(x + d, 4)))
-            )
-
-    for n, (buf, out) in enumerate(((gr_v, gg_o), (ur_v, gu_o))):
-        for one in row_shares[3 * n : 3 * n + 3]:
-            one.wait_recv()
+    g_rest = g_rest + pass_rows(g_sender, g_first)
+    u_sender, u_first, u_rest = share_rows(20, ur_v)
+    for one in g_rest:
+        one.wait_recv()
+
+    def weight_grad(buf, target, out, n):
         for b in range(2):
             for part in range(3):
                 tall = slice(part * 256, (part + 1) * 256)
-                target = td_v.at[1] if n == 0 else sg_v
                 target[tall, b * NAR : (b + 1) * NAR] = tn(buf[:, tall], s_x[b]).astype(BF)
-        done = pltpu.make_async_copy(td_v.at[1] if n == 0 else sg_v, out.at[0], out_sem.at[2 + n])
+        done = pltpu.make_async_copy(target, out.at[0], out_sem.at[n])
         done.start()
-        if n == 0:
-            out_gg = done
-        else:
-            out_gu = done
+        return done
+
+    u_rest = u_rest + pass_rows(u_sender, u_first)
+    out_gg = weight_grad(gr_v, td_v.at[1], gg_o, 2)
+    for one in u_rest:
+        one.wait_recv()
+    out_gu = weight_grad(ur_v, sg_v, gu_o, 3)
 
     all_sent(0, s_x.at[0, pl.ds(0, SR - 2 * SLOT)])
     all_sent(1, t_back.at[pl.ds(0, TR - SLOT)])
@@ -472,14 +551,16 @@
             buf(HID, COL),
             buf(HID, COL),
             buf(2, HID, NAR),
-            buf(TOK, TR),
-            buf(TOK, TR),
+            buf(TR, TOK),
+            buf(TR, TOK),
+            buf(4, TR, TOK),
             buf(4, TOK, TR),
             buf(2, TR, NAR),
             buf(TR, COL),
             buf(2, SR, NAR),
             buf(2, TR, COL),
             buf(3, 2, HALF, HID),
+            buf(2, HALF, HID, dtype=F32),
             buf(2, HALF, HID, dtype=F32),
             buf(3, 2, HALF, HID),
             buf(2, HALF, HID),
@@ -500,6 +581,7 @@
             buf(2, SR, NAR),
             buf(3, HALF, HID),
             buf(HALF, HID, dtype=F32),
+            buf(HALF, HID, dtype=F32),
             buf(3, HALF, HID),
             buf(SR, HID),
             buf(SR, HID),
@@ -507,10 +589,10 @@
             dma((4,)),
             dma((5,)),
             dma((5,)),
-            dma((12,)),
-            dma((12,)),
-            dma((20,)),
-            dma((20,)),
+            dma((16,)),
+            dma((16,)),
+            dma((26,)),
+            dma((26,)),
         ],
         compiler_params=pltpu.CompilerParams(
             collective_id=0, has_side_effects=True, vmem_limit_bytes=60 << 20
@@ -519,7 +601,7 @@
             flops=16_000_000_000, bytes_accessed=24_000_000, transcendentals=1_000_000
         ),
         name="distill",
-    )(ids, gates, order.reshape(1, OWNERS), tokens, tg, tu, td, sg, su, sd)
+    )(ids.T, gates.T, order.reshape(1, OWNERS), tokens, tg, tu, td, sg, su, sd)
 
 
 def solution(mesh):

time: 229 us -> 205 us (0.90)
  Pallas kernels: 217 us -> 196 us
  local copies, waits for them, and re-layouts: 10.2 us -> 7.3 us
    pallas_call x1, Pallas kernels: 217 us -> 196 us  [shards(): pl.pallas_call(body, out_shape=(jax.ShapeDtypeStruct((TOK, COL), F32), ja...]
    unnamed x12 -> x10, local copies, waits for them, and re-layouts: 10.2 us -> 7.3 us
where the time goes in v2:
time: 205 us; the launch traced here: 204 us
  Pallas kernels  196 us (96%)
  local copies, waits for them, and re-layouts  7.3 us (4%)
    pallas_call x1, Pallas kernels, shards(): pl.pallas_call(body, out_shape=(jax.ShapeDtypeStruct((TOK, COL), F32), ja...  196 us
    unnamed x10, local copies, waits for them, and re-layouts  7.3 us

profile of v2, /device:TPU:1, one launch (start us, length us, event | category | flops | bytes accessed | tf_op | source)
XLA Modules:
  0.0 203.8 jit_solution(158239593124624480)
XLA Ops:
  0.6 195.8 %distill.1 = (f32[192,1024]{1,0:T(8,128)}, bf16[1,768,1024]{2,1,0:T(8,128)(2,1)}, bf16[1,768,1024]{2,1,0:T(8,128)(2,1)}, bf16[1,768,1024]{2,1,0:T(8,128)(2,1)}) custom-call(s32[8,192]{1,0:T(8,128)} %bitcast.3, f32[8,192]{1,0:T(8,128)} %bitcast.4, s32[1,32]{1,0:T(1,128)} %bitcast.5, bf16[192,2048]{1,0:T(8,128)(2,1)} %tokens.1, bf16[1,768,2048]{2,1,0:T(8,128)(2,1)} %tg.1, ...), custom_call_target="tpu_custom_call" | custom-call | flops 16000000000 | bytes 24000000 | tf_op jit(solution)/shard_map/distill/pallas_call | solution.py:536
  196.5 0.0 copy-start.2
  196.5 2.2 %copy.18 = f32[192,1024]{1,0:T(8,128)} copy(f32[192,1024]{1,0:T(8,128)} %get-tuple-element.8) | data formatting | bytes 1572864
  198.7 0.0 copy-done.2
  198.7 0.0 copy-start.1
  198.7 1.1 copy.19
  199.8 0.8 copy-done.1
  200.6 0.0 copy-start
  200.7 1.1 copy.20
  201.8 0.8 copy-done
  202.6 1.1 copy.21
Async XLA Ops:
  196.5 2.2 %copy-start.2 = (bf16[1,768,1024]{2,1,0:T(8,128)(2,1)S(1)}, bf16[1,768,1024]{2,1,0:T(8,128)(2,1)}, u32[]{:S(2)}) copy-start(bf16[1,768,1024]{2,1,0:T(8,128)(2,1)} %get-tuple-element.9) | copy-start | bytes 4718596
  198.7 2.0 copy-start.1
  200.6 2.0 copy-start

commit v3 on v2

--- a/solution.py
+++ b/solution.py
@@ -14,6 +14,7 @@
 TR = OWNERS * SLOT
 SR = 2 * TR
 HALF = SR // 4
+PACK = HALF // SLOT * (SLOT - 1)
 HID = 768
 COL = 1024
 NAR = 512
@@ -49,8 +50,9 @@
     sd,
     res_o,
     gg_o,
-    gu_o,
     gd_o,
+    ur_o,
+    sc_o,
     tok_v,
     tg_v,
     tu_v,
@@ -65,7 +67,10 @@
     s_send,
     t_send,
     s_x,
+    s_c,
     t_x,
+    pack,
+    unpack,
     s_psend,
     s_pown,
     s_pkeep,
@@ -86,6 +91,7 @@
     res_v,
     g_send,
     g_x,
+    g_c,
     b_send,
     b_own,
     b_keep,
@@ -166,14 +172,14 @@
     ).astype(F32).astype(BF)
     rank = (member * nn(member.astype(BF), upto)).astype(BF)
     spread = (
-        lax.broadcasted_iota(jnp.int32, (TR, OWNERS), 0) // SLOT
+        lax.shift_right_logical(lax.broadcasted_iota(jnp.int32, (TR, OWNERS), 0), 4)
         == lax.broadcasted_iota(jnp.int32, (TR, OWNERS), 1)
     ).astype(F32).astype(BF)
     turn = (
         lax.broadcasted_iota(jnp.int32, (OWNERS, OWNERS), 0) == order[0:1, :]
     ).astype(F32).astype(BF)
     s_spread = nt(spread, turn).astype(BF)
-    want = (lax.rem(lax.broadcasted_iota(jnp.int32, (TR, TOK), 0), SLOT) + 1).astype(F32)
+    want = ((lax.broadcasted_iota(jnp.int32, (TR, 1), 0) & (SLOT - 1)) + 1).astype(F32)
     s_hit = nn(s_spread, rank) == want
     s_onehot[...] = jnp.where(s_hit, 1.0, 0.0).astype(BF)
     loads[0].wait()
@@ -244,6 +250,22 @@
     for n in range(4):
         comb_t[n] = nt(same_token, comb[n]).astype(BF)
 
+    def packed_place(shape, dim):
+        slot = lax.broadcasted_iota(jnp.int32, shape, dim)
+        inner = slot & (SLOT - 1)
+        to = lax.shift_right_logical(slot, 4) * (SLOT - 1) + inner
+        hit = (to == lax.broadcasted_iota(jnp.int32, shape, 1 - dim)) & (inner < SLOT - 1)
+        return jnp.where(hit, 1.0, 0.0).astype(BF)
+
+    pack[...] = packed_place((PACK, HALF), 1)
+    unpack[...] = packed_place((HALF, PACK), 0)
+
+    def packed(block):
+        return nn(pack[...], block).astype(BF)
+
+    def unpacked(block):
+        return nn(unpack[...], block).astype(BF)
+
     def to_core(n, src, dst):
         return pltpu.make_async_remote_copy(
             src_ref=src,
@@ -279,20 +301,24 @@
         swaps.append(go(to_core(i, s_x.at[r, block], s_x.at[r, block])))
     loads[1].wait()
     loads[2].wait()
-    across_sums = []
     for i, q in enumerate(order_of_shares):
         swaps[i].wait_recv()
-        block = rows(q, HALF)
+        block, small = rows(q, HALF), rows(q, PACK)
+        for b in range(2):
+            s_c[b, small, :] = packed(s_x[b, block, :])
         for n, w in enumerate((sg_v, su_v)):
-            total = nt(s_x[0, block, :], w[:, :NAR]) + nt(s_x[1, block, :], w[:, NAR:])
+            total = nt(s_c[0, small, :], w[:, :NAR]) + nt(s_c[1, small, :], w[:, NAR:])
             if i < 2:
                 s_psend[i, n] = total.astype(BF)
             elif i == 2:
                 s_pkeep[n] = total
             else:
                 s_pown[n] = total
-        if i < 2:
-            across_sums.append(go(to_ring(i, s_psend.at[i], s_precv.at[i], across)))
+        if i == 0:
+            first_sum = go(to_ring(0, s_psend.at[0], s_precv.at[0], across))
+
+    out_sc = pltpu.make_async_copy(s_c, sc_o, out_sem.at[3])
+    out_sc.start()
 
     all_here(1, t_x.at[0, pl.ds(0, TR - SLOT)])
     t_swaps = []
@@ -304,8 +330,9 @@
     for i, half in enumerate((1 - g, g)):
         t_swaps[i].wait_recv()
         block = rows(half, HALF)
+        t_rows_a, t_rows_b = packed(t_x[0, block, :]), packed(t_x[1, block, :])
         for n, w in enumerate((tg_v, tu_v)):
-            total = nt(t_x[0, block, :], w[:, :COL]) + nt(t_x[1, block, :], w[:, COL:])
+            total = nt(t_rows_a, w[:, :COL]) + nt(t_rows_b, w[:, COL:])
             if i == 0:
                 t_psend[n] = total.astype(BF)
             else:
@@ -321,15 +348,16 @@
                     device_id_type=MESH,
                 )
             )
-    across_sums[0].wait_recv()
+    first_sum.wait_recv()
+    across_sum = go(to_ring(1, s_psend.at[1], s_precv.at[1], across))
     for n in range(2):
         s_psend[2, n] = (s_pkeep[n] + s_precv[0, n].astype(F32)).astype(BF)
     near_sum = go(to_ring(2, s_psend.at[2], s_precv.at[2], near))
     t_pre.wait_recv()
     t_gate = t_pown[0] + t_precv[0].astype(F32)
     t_up = t_pown[1] + t_precv[1].astype(F32)
-    own_half = rows(g, HALF)
-    other_half = rows(1 - g, HALF)
+    own_half = rows(g, PACK)
+    other_half = rows(1 - g, PACK)
     t_hid[own_half, :] = (t_gate * jax.nn.sigmoid(t_gate) * t_up).astype(BF)
     t_share = go(
         pltpu.make_async_remote_copy(
@@ -349,17 +377,18 @@
 
     def teacher_back(half, one):
         one.wait_recv()
-        block = rows(half, HALF)
-        t_ret[block, :] = (nn(t_hid[block, :], td_v[r]) + t_crecv[block, :].astype(F32)).astype(BF)
+        block = rows(half, PACK)
+        total = nn(t_hid[block, :], td_v[r]) + t_crecv[block, :].astype(F32)
+        t_ret[rows(half, HALF), :] = unpacked(total.astype(BF))
         for q in (2 * half, 2 * half + 1):
             scatter_share(2, q, lambda e: t_ret.at[rows(place(e), SLOT)], t_back.at[rows(me, SLOT)])
 
-    across_sums[1].wait_recv()
+    across_sum.wait_recv()
     near_sum.wait_recv()
     for n in range(2):
         s_pown[n] = s_pown[n] + s_precv[1, n].astype(F32) + s_precv[2, n].astype(F32)
     s_gate, s_up = s_pown[0], s_pown[1]
-    own_share = rows(x, HALF)
+    own_share = rows(x, PACK)
     s_hid[own_share, :] = (s_gate * jax.nn.sigmoid(s_gate) * s_up).astype(BF)
     own_hidden = s_hid.at[own_share]
     to_near = go(to_ring(3, own_hidden, own_hidden, near))
@@ -370,14 +399,15 @@
     s_outs = []
 
     def merged_part(i, q):
-        block = rows(q, HALF)
+        block = rows(q, PACK)
         s_csend[block, :] = nn(s_hid[block, :], sd_v[nr]).astype(BF)
         s_outs.append(go(to_core(8 + i, s_csend.at[block], s_crecv.at[block])))
 
     def merged_back(i, q):
         s_outs[i].wait_recv()
-        block = rows(q, HALF)
-        s_ret[block, :] = (nn(s_hid[block, :], sd_v[r]) + s_crecv[block, :].astype(F32)).astype(BF)
+        block = rows(q, PACK)
+        total = nn(s_hid[block, :], sd_v[r]) + s_crecv[block, :].astype(F32)
+        s_ret[rows(q, HALF), :] = unpacked(total.astype(BF))
         scatter_share(
             3, q, lambda e: s_ret.at[rows(place(e), 2 * SLOT)], s_back.at[h, m_rows]
         )
@@ -390,16 +420,16 @@
     teacher_back(1 - g, t_outs[1])
     t_back[rows(me, SLOT), :] = t_ret[t_rows, :]
     to_near.wait_recv()
-    near_hidden = s_hid.at[rows(near, HALF)]
+    near_hidden = s_hid.at[rows(near, PACK)]
     passed_on = go(to_ring(5, near_hidden, near_hidden, across))
     merged_part(1, near)
-    merged_back(0, x)
     to_across.wait_recv()
     merged_part(2, across)
+    passed_on.wait_recv()
+    merged_part(3, opposite)
+    merged_back(0, x)
     merged_back(1, near)
     merged_back(2, across)
-    passed_on.wait_recv()
-    merged_part(3, opposite)
     merged_back(3, opposite)
     s_back[h, m_rows, :] = s_ret[s_rows, :]
 
@@ -430,22 +460,24 @@
     for i, q in enumerate(order_of_shares):
         block = rows(q, HALF)
         swaps.append(go(to_core(12 + i, g_x.at[r, block], g_x.at[r, block])))
-    top, low = pl.ds(0, HALF // 2), pl.ds(HALF // 2, HALF // 2)
+    top, low = pl.ds(0, 128), pl.ds(128, PACK - 128)
     for i, q in enumerate(order_of_shares):
         swaps[i].wait_recv()
-        block = rows(q, HALF)
-        total = nt(g_x[0, block, :], sd_v[0]) + nt(g_x[1, block, :], sd_v[1])
+        block, small = rows(q, HALF), rows(q, PACK)
+        for b in range(2):
+            g_c[b, small, :] = packed(g_x[b, block, :])
+        total = nt(g_c[0, small, :], sd_v[0]) + nt(g_c[1, small, :], sd_v[1])
         if i == 0:
             b_send[0] = total.astype(BF)
             from_left = go(to_ring(6, b_send.at[0, top], b_recv.at[0, top], right))
             from_right = go(to_ring(7, b_send.at[0, low], b_recv.at[0, low], left))
         elif i == 1:
-            b_send[1, low, :] = total[HALF // 2 :].astype(BF)
-            b_keep[top, :] = total[: HALF // 2]
+            b_send[1, low, :] = total[128:].astype(BF)
+            b_keep[top, :] = total[:128]
             left_low = go(to_ring(8, b_send.at[1, low], b_recv.at[1, low], right))
         elif i == 2:
-            b_send[2, top, :] = total[: HALF // 2].astype(BF)
-            b_keep[low, :] = total[HALF // 2 :]
+            b_send[2, top, :] = total[:128].astype(BF)
+            b_keep[low, :] = total[128:]
             right_top = go(to_ring(9, b_send.at[2, top], b_recv.at[2, top], left))
         else:
             b_own[...] = total
@@ -453,7 +485,7 @@
     def down_grad(b):
         for part in range(3):
             tall = slice(part * 256, (part + 1) * 256)
-            td_v[0, tall, b * NAR : (b + 1) * NAR] = tn(s_hid[:, tall], g_x[b]).astype(BF)
+            td_v[0, tall, b * NAR : (b + 1) * NAR] = tn(s_hid[:, tall], g_c[b]).astype(BF)
 
     down_grad(0)
     from_left.wait_recv()
@@ -463,7 +495,7 @@
     b_send[2, low, :] = (b_keep[low, :] + b_recv[0, low, :].astype(F32)).astype(BF)
     right_low = go(to_ring(11, b_send.at[2, low], b_recv.at[2, low], left))
     down_grad(1)
-    out_gd = pltpu.make_async_copy(td_v.at[0], gd_o.at[0], out_sem.at[1])
+    out_gd = pltpu.make_async_copy(td_v.at[0], gd_o, out_sem.at[1])
     out_gd.start()
 
     for one in (left_low, right_top, left_top, right_low):
@@ -473,7 +505,7 @@
     sig = jax.nn.sigmoid(s_gate)
 
     def part_of(q, lower):
-        return pl.ds(pl.multiple_of(q * HALF + lower * (HALF // 2), HALF // 2), HALF // 2)
+        return pl.ds(pl.multiple_of(q * PACK + lower * 128, SLOT), PACK - 128 if lower else 128)
 
     def share_rows(n, buf):
         def send(i, q, lower, p):
@@ -499,20 +531,17 @@
     for one in g_rest:
         one.wait_recv()
 
-    def weight_grad(buf, target, out, n):
-        for b in range(2):
-            for part in range(3):
-                tall = slice(part * 256, (part + 1) * 256)
-                target[tall, b * NAR : (b + 1) * NAR] = tn(buf[:, tall], s_x[b]).astype(BF)
-        done = pltpu.make_async_copy(target, out.at[0], out_sem.at[n])
-        done.start()
-        return done
-
     u_rest = u_rest + pass_rows(u_sender, u_first)
-    out_gg = weight_grad(gr_v, td_v.at[1], gg_o, 2)
+    for b in range(2):
+        for part in range(3):
+            tall = slice(part * 256, (part + 1) * 256)
+            td_v[1, tall, b * NAR : (b + 1) * NAR] = tn(gr_v[:, tall], s_c[b]).astype(BF)
+    out_gg = pltpu.make_async_copy(td_v.at[1], gg_o, out_sem.at[2])
+    out_gg.start()
     for one in u_rest:
         one.wait_recv()
-    out_gu = weight_grad(ur_v, sg_v, gu_o, 3)
+    out_ur = pltpu.make_async_copy(ur_v, ur_o, out_sem.at[4])
+    out_ur.start()
 
     all_sent(0, s_x.at[0, pl.ds(0, SR - 2 * SLOT)])
     all_sent(1, t_back.at[pl.ds(0, TR - SLOT)])
@@ -521,7 +550,31 @@
     all_sent(4, s_x.at[0, pl.ds(0, SR - 2 * SLOT)])
     for one in pending:
         one.wait_send()
-    for one in (out_res, out_gd, out_gg, out_gu):
+    for one in (out_res, out_gd, out_gg, out_ur, out_sc):
+        one.wait()
+
+
+def finish(res, gg, gd, ur, sc, res_o, gg_o, gu_o, gd_o, ur_v, sc_v, gu_v, gg_v, gd_v, res_v, sem):
+    def copy(n, src, dst):
+        one = pltpu.make_async_copy(src, dst, sem.at[n])
+        one.start()
+        return one
+
+    loads = [copy(0, ur, ur_v), copy(1, sc.at[0], sc_v.at[0]), copy(2, sc.at[1], sc_v.at[1])]
+    through = [copy(3, gg, gg_v), copy(4, gd, gd_v), copy(5, res, res_v)]
+    rest = []
+    loads[0].wait()
+    for b in range(2):
+        loads[1 + b].wait()
+        for part in range(3):
+            tall = slice(part * 256, (part + 1) * 256)
+            gu_v[b, tall, :] = tn(ur_v[:, tall], sc_v[b]).astype(BF)
+        rest.append(copy(6 + b, gu_v.at[b], gu_o.at[0, :, pl.ds(b * NAR, NAR)]))
+        if b == 0:
+            for n, (held, out) in enumerate(((gg_v, gg_o.at[0]), (gd_v, gd_o.at[0]), (res_v, res_o))):
+                through[n].wait()
+                rest.append(copy(8 + n, held, out))
+    for one in rest:
         one.wait()
 
 
@@ -533,16 +586,17 @@
     def buf(*shape, dtype=BF):
         return pltpu.VMEM(shape, dtype)
 
-    return pl.pallas_call(
+    parts = pl.pallas_call(
         body,
         out_shape=(
             jax.ShapeDtypeStruct((TOK, COL), F32),
-            jax.ShapeDtypeStruct((1, HID, COL), BF),
-            jax.ShapeDtypeStruct((1, HID, COL), BF),
-            jax.ShapeDtypeStruct((1, HID, COL), BF),
+            jax.ShapeDtypeStruct((HID, COL), BF),
+            jax.ShapeDtypeStruct((HID, COL), BF),
+            jax.ShapeDtypeStruct((4 * PACK, HID), BF),
+            jax.ShapeDtypeStruct((2, 4 * PACK, NAR), BF),
         ),
         in_specs=[vmem] * 3 + [hbm] * 7,
-        out_specs=(hbm,) * 4,
+        out_specs=(hbm,) * 5,
         scratch_shapes=[
             buf(TOK, COL),
             buf(HID, 2 * COL),
@@ -558,35 +612,39 @@
             buf(2, TR, NAR),
             buf(TR, COL),
             buf(2, SR, NAR),
+            buf(2, 4 * PACK, NAR),
             buf(2, TR, COL),
-            buf(3, 2, HALF, HID),
-            buf(2, HALF, HID, dtype=F32),
-            buf(2, HALF, HID, dtype=F32),
-            buf(3, 2, HALF, HID),
-            buf(2, HALF, HID),
-            buf(2, HALF, HID, dtype=F32),
-            buf(2, HALF, HID),
-            buf(SR, HID),
-            buf(TR, HID),
+            buf(PACK, HALF),
+            buf(HALF, PACK),
+            buf(3, 2, PACK, HID),
+            buf(2, PACK, HID, dtype=F32),
+            buf(2, PACK, HID, dtype=F32),
+            buf(3, 2, PACK, HID),
+            buf(2, PACK, HID),
+            buf(2, PACK, HID, dtype=F32),
+            buf(2, PACK, HID),
+            buf(4 * PACK, HID),
+            buf(2 * PACK, HID),
+            buf(2 * PACK, COL),
+            buf(2 * PACK, COL),
             buf(TR, COL),
             buf(TR, COL),
-            buf(TR, COL),
-            buf(TR, COL),
-            buf(SR, NAR),
-            buf(SR, NAR),
+            buf(4 * PACK, NAR),
+            buf(4 * PACK, NAR),
             buf(SR, NAR),
             buf(2, TR, NAR),
             buf(TOK, COL, dtype=F32),
             buf(2, TR, NAR),
             buf(2, SR, NAR),
-            buf(3, HALF, HID),
-            buf(HALF, HID, dtype=F32),
-            buf(HALF, HID, dtype=F32),
-            buf(3, HALF, HID),
-            buf(SR, HID),
-            buf(SR, HID),
+            buf(2, 4 * PACK, NAR),
+            buf(3, PACK, HID),
+            buf(PACK, HID, dtype=F32),
+            buf(PACK, HID, dtype=F32),
+            buf(3, PACK, HID),
+            buf(4 * PACK, HID),
+            buf(4 * PACK, HID),
             dma((9,)),
-            dma((4,)),
+            dma((5,)),
             dma((5,)),
             dma((5,)),
             dma((16,)),
@@ -602,6 +660,27 @@
         ),
         name="distill",
     )(ids.T, gates.T, order.reshape(1, OWNERS), tokens, tg, tu, td, sg, su, sd)
+    weight = jax.ShapeDtypeStruct((1, HID, COL), BF)
+    return pl.pallas_call(
+        finish,
+        out_shape=(jax.ShapeDtypeStruct((TOK, COL), F32), weight, weight, weight),
+        in_specs=[hbm] * 5,
+        out_specs=(hbm,) * 4,
+        scratch_shapes=[
+            buf(4 * PACK, HID),
+            buf(2, 4 * PACK, NAR),
+            buf(2, HID, NAR),
+            buf(HID, COL),
+            buf(HID, COL),
+            buf(TOK, COL, dtype=F32),
+            dma((11,)),
+        ],
+        compiler_params=pltpu.CompilerParams(vmem_limit_bytes=60 << 20),
+        cost_estimate=pl.CostEstimate(
+            flops=1_600_000_000, bytes_accessed=13_000_000, transcendentals=0
+        ),
+        name="finish",
+    )(*parts)
 
 
 def solution(mesh):

time: 205 us -> 194 us (0.946)
  local copies, waits for them, and re-layouts: 7.3 us -> 0 us
  Pallas kernels: 196 us -> 193 us
    pallas_call x1, Pallas kernels: 196 us -> 188 us  [shards(): pl.pallas_call(body, out_shape=(jax.ShapeDtypeStruct((TOK, COL), F32), ja...]
    unnamed x10 -> x0, local copies, waits for them, and re-layouts: 7.3 us -> none
    pallas_call x0 -> x1, Pallas kernels: none -> 5.19 us  [shards(): pl.pallas_call(finish, out_shape=(jax.ShapeDtypeStruct((TOK, COL), F32),...]
where the time goes in v3:
time: 194 us
  Pallas kernels  193 us (99%)
    pallas_call x1, Pallas kernels, shards(): pl.pallas_call(body, out_shape=(jax.ShapeDtypeStruct((TOK, COL), F32), ja...  188 us
    pallas_call x1, Pallas kernels, shards(): pl.pallas_call(finish, out_shape=(jax.ShapeDtypeStruct((TOK, COL), F32),...  5.19 us

profile of v3, /device:TPU:1, one launch (start us, length us, event | category | flops | bytes accessed | tf_op | source)
XLA Modules:
  0.0 193.5 jit_solution(1828607314230293292)
XLA Ops:
  0.6 187.5 %distill.1 = (f32[192,1024]{1,0:T(8,128)}, bf16[768,1024]{1,0:T(8,128)(2,1)}, bf16[768,1024]{1,0:T(8,128)(2,1)}, bf16[960,768]{1,0:T(8,128)(2,1)}, bf16[2,960,512]{2,1,0:T(8,128)(2,1)}) custom-call(s32[8,192]{1,0:T(8,128)} %bitcast.3, f32[8,192]{1,0:T(8,128)} %bitcast.4, s32[1,32]{1,0:T(1,128)} %bitcast.5, bf16[192,2048]{1,0:T(8,128)(2,1)} %tokens.1, ...), custom_call_target="tpu_custom_call" | custom-call | flops 16000000000 | bytes 24000000 | tf_op jit(solution)/shard_map/distill/pallas_call | solution.py:589
  188.2 5.2 %finish.1 = (f32[192,1024]{1,0:T(8,128)}, bf16[1,768,1024]{2,1,0:T(8,128)(2,1)}, bf16[1,768,1024]{2,1,0:T(8,128)(2,1)}, bf16[1,768,1024]{2,1,0:T(8,128)(2,1)}) custom-call(f32[192,1024]{1,0:T(8,128)} %get-tuple-element.9.res, bf16[768,1024]{1,0:T(8,128)(2,1)} %get-tuple-element.10.gg, bf16[768,1024]{1,0:T(8,128)(2,1)} %get-tuple-element.11.gd, ...), custom_call_target="tpu_custom_call" | custom-call | flops 1600000000 | bytes 13000000 | tf_op jit(solution)/shard_map/finish/pallas_call | solution.py:664

commit v4 on v3

--- a/solution.py
+++ b/solution.py
@@ -383,6 +383,25 @@
         for q in (2 * half, 2 * half + 1):
             scatter_share(2, q, lambda e: t_ret.at[rows(place(e), SLOT)], t_back.at[rows(me, SLOT)])
 
+    def part_of(q, lower):
+        return pl.ds(pl.multiple_of(q * PACK + lower * 128, SLOT), PACK - 128 if lower else 128)
+
+    def share_rows(n, buf):
+        def send(i, q, lower, p):
+            block = buf.at[part_of(q, lower)]
+            return go(to_ring(n + i, block, block, p))
+
+        return send, [send(0, x, 0, right), send(1, x, 1, left)], [
+            send(2, x, 1, right),
+            send(3, x, 0, left),
+        ]
+
+    def pass_rows(send, first):
+        first[0].wait_recv()
+        one = send(4, left, 0, right)
+        first[1].wait_recv()
+        return [one, send(5, right, 1, left)]
+
     across_sum.wait_recv()
     near_sum.wait_recv()
     for n in range(2):
@@ -390,9 +409,7 @@
     s_gate, s_up = s_pown[0], s_pown[1]
     own_share = rows(x, PACK)
     s_hid[own_share, :] = (s_gate * jax.nn.sigmoid(s_gate) * s_up).astype(BF)
-    own_hidden = s_hid.at[own_share]
-    to_near = go(to_ring(3, own_hidden, own_hidden, near))
-    to_across = go(to_ring(4, own_hidden, own_hidden, across))
+    h_sender, h_first, h_rest = share_rows(26, s_hid)
 
     loads[5].wait()
     loads[6].wait()
@@ -416,16 +433,16 @@
     t_csend[other_half, :] = nn(t_hid[other_half, :], td_v[nr]).astype(BF)
     t_outs.append(go(to_core(7, t_csend.at[other_half], t_crecv.at[other_half])))
     merged_part(0, x)
+    h_far = pass_rows(h_sender, h_first)
     teacher_back(g, t_outs[0])
     teacher_back(1 - g, t_outs[1])
     t_back[rows(me, SLOT), :] = t_ret[t_rows, :]
-    to_near.wait_recv()
-    near_hidden = s_hid.at[rows(near, PACK)]
-    passed_on = go(to_ring(5, near_hidden, near_hidden, across))
+    for one in h_rest:
+        one.wait_recv()
     merged_part(1, near)
-    to_across.wait_recv()
     merged_part(2, across)
-    passed_on.wait_recv()
+    for one in h_far:
+        one.wait_recv()
     merged_part(3, opposite)
     merged_back(0, x)
     merged_back(1, near)
@@ -503,25 +520,6 @@
     back = b_own[...] + b_recv[1].astype(F32) + b_recv[2].astype(F32)
     s_gate, s_up = s_pown[0], s_pown[1]
     sig = jax.nn.sigmoid(s_gate)
-
-    def part_of(q, lower):
-        return pl.ds(pl.multiple_of(q * PACK + lower * 128, SLOT), PACK - 128 if lower else 128)
-
-    def share_rows(n, buf):
-        def send(i, q, lower, p):
-            block = buf.at[part_of(q, lower)]
-            return go(to_ring(n + i, block, block, p))
-
-        return send, [send(0, x, 0, right), send(1, x, 1, left)], [
-            send(2, x, 1, right),
-            send(3, x, 0, left),
-        ]
-
-    def pass_rows(send, first):
-        first[0].wait_recv()
-        one = send(4, left, 0, right)
-        first[1].wait_recv()
-        return [one, send(5, right, 1, left)]
 
     gr_v[own_share, :] = (back * s_up * sig * (1.0 + s_gate * (1.0 - sig))).astype(BF)
     g_sender, g_first, g_rest = share_rows(14, gr_v)
@@ -649,8 +647,8 @@
             dma((5,)),
             dma((16,)),
             dma((16,)),
-            dma((26,)),
-            dma((26,)),
+            dma((32,)),
+            dma((32,)),
         ],
         compiler_params=pltpu.CompilerParams(
             collective_id=0, has_side_effects=True, vmem_limit_bytes=60 << 20

time: 194 us -> 190 us (0.979)
  Pallas kernels: 193 us -> 189 us
    pallas_call x1, Pallas kernels: 188 us -> 184 us  [shards(): pl.pallas_call(body, out_shape=(jax.ShapeDtypeStruct((TOK, COL), F32), ja...]
where the time goes in v4:
time: 190 us
  Pallas kernels  189 us (99%)
    pallas_call x1, Pallas kernels, shards(): pl.pallas_call(body, out_shape=(jax.ShapeDtypeStruct((TOK, COL), F32), ja...  184 us
    pallas_call x1, Pallas kernels, shards(): pl.pallas_call(finish, out_shape=(jax.ShapeDtypeStruct((TOK, COL), F32),...  5.18 us

profile of v4, /device:TPU:1, one launch (start us, length us, event | category | flops | bytes accessed | tf_op | source)
XLA Modules:
  0.0 189.9 jit_solution(9446963147729633635)
XLA Ops:
  0.6 183.9 %distill.1 = (f32[192,1024]{1,0:T(8,128)}, bf16[768,1024]{1,0:T(8,128)(2,1)}, bf16[768,1024]{1,0:T(8,128)(2,1)}, bf16[960,768]{1,0:T(8,128)(2,1)}, bf16[2,960,512]{2,1,0:T(8,128)(2,1)}) custom-call(s32[8,192]{1,0:T(8,128)} %bitcast.3, f32[8,192]{1,0:T(8,128)} %bitcast.4, s32[1,32]{1,0:T(1,128)} %bitcast.5, bf16[192,2048]{1,0:T(8,128)(2,1)} %tokens.1, ...), custom_call_target="tpu_custom_call" | custom-call | flops 16000000000 | bytes 24000000 | tf_op jit(solution)/shard_map/distill/pallas_call | solution.py:587
  184.6 5.2 %finish.1 = (f32[192,1024]{1,0:T(8,128)}, bf16[1,768,1024]{2,1,0:T(8,128)(2,1)}, bf16[1,768,1024]{2,1,0:T(8,128)(2,1)}, bf16[1,768,1024]{2,1,0:T(8,128)(2,1)}) custom-call(f32[192,1024]{1,0:T(8,128)} %get-tuple-element.9.res, bf16[768,1024]{1,0:T(8,128)(2,1)} %get-tuple-element.10.gg, bf16[768,1024]{1,0:T(8,128)(2,1)} %get-tuple-element.11.gd, ...), custom_call_target="tpu_custom_call" | custom-call | flops 1600000000 | bytes 13000000 | tf_op jit(solution)/shard_map/finish/pallas_call | solution.py:662

commit v5 on v4

--- a/solution.py
+++ b/solution.py
@@ -434,9 +434,6 @@
     t_outs.append(go(to_core(7, t_csend.at[other_half], t_crecv.at[other_half])))
     merged_part(0, x)
     h_far = pass_rows(h_sender, h_first)
-    teacher_back(g, t_outs[0])
-    teacher_back(1 - g, t_outs[1])
-    t_back[rows(me, SLOT), :] = t_ret[t_rows, :]
     for one in h_rest:
         one.wait_recv()
     merged_part(1, near)
@@ -444,6 +441,9 @@
     for one in h_far:
         one.wait_recv()
     merged_part(3, opposite)
+    teacher_back(g, t_outs[0])
+    teacher_back(1 - g, t_outs[1])
+    t_back[rows(me, SLOT), :] = t_ret[t_rows, :]
     merged_back(0, x)
     merged_back(1, near)
     merged_back(2, across)

time: 190 us -> 195 us (1.026)
  Pallas kernels: 189 us -> 194 us
    pallas_call x1, Pallas kernels: 184 us -> 189 us  [shards(): pl.pallas_call(body, out_shape=(jax.ShapeDtypeStruct((TOK, COL), F32), ja...]
where the time goes in v5:
time: 195 us
  Pallas kernels  194 us (99%)
    pallas_call x1, Pallas kernels, shards(): pl.pallas_call(body, out_shape=(jax.ShapeDtypeStruct((TOK, COL), F32), ja...  189 us
    pallas_call x1, Pallas kernels, shards(): pl.pallas_call(finish, out_shape=(jax.ShapeDtypeStruct((TOK, COL), F32),...  5.18 us

profile of v5, /device:TPU:1, one launch (start us, length us, event | category | flops | bytes accessed | tf_op | source)
XLA Modules:
  0.0 194.5 jit_solution(11563317802757294184)
XLA Ops:
  0.6 188.5 %distill.1 = (f32[192,1024]{1,0:T(8,128)}, bf16[768,1024]{1,0:T(8,128)(2,1)}, bf16[768,1024]{1,0:T(8,128)(2,1)}, bf16[960,768]{1,0:T(8,128)(2,1)}, bf16[2,960,512]{2,1,0:T(8,128)(2,1)}) custom-call(s32[8,192]{1,0:T(8,128)} %bitcast.3, f32[8,192]{1,0:T(8,128)} %bitcast.4, s32[1,32]{1,0:T(1,128)} %bitcast.5, bf16[192,2048]{1,0:T(8,128)(2,1)} %tokens.1, ...), custom_call_target="tpu_custom_call" | custom-call | flops 16000000000 | bytes 24000000 | tf_op jit(solution)/shard_map/distill/pallas_call | solution.py:587
  189.2 5.2 %finish.1 = (f32[192,1024]{1,0:T(8,128)}, bf16[1,768,1024]{2,1,0:T(8,128)(2,1)}, bf16[1,768,1024]{2,1,0:T(8,128)(2,1)}, bf16[1,768,1024]{2,1,0:T(8,128)(2,1)}) custom-call(f32[192,1024]{1,0:T(8,128)} %get-tuple-element.9.res, bf16[768,1024]{1,0:T(8,128)(2,1)} %get-tuple-element.10.gg, bf16[768,1024]{1,0:T(8,128)(2,1)} %get-tuple-element.11.gd, ...), custom_call_target="tpu_custom_call" | custom-call | flops 1600000000 | bytes 13000000 | tf_op jit(solution)/shard_map/finish/pallas_call | solution.py:662
